TPU v7x, 128 devices: a whole 4x4x4 slice. The times are simulated.
128 devices in a mesh: dom: 128 (over z, x, y, core).
Axes of the slice: x: 4, y: 4, z: 4, core: 2. Of those that a mesh axis runs over, the one named last changes fastest.
Arguments:
- features: bfloat16 [1048576, 128], P('dom'), may hold values from -5000 to 5000
- teacher_w: bfloat16 [128, 172], replicated, may hold values from -1.5 to 1.5
- teacher_b: float32 [172], replicated, may hold values from -4 to 4
- ema_prior: float32 [172], replicated, may hold values from 0.001 to 0.02
- target_prior: float32 [172], replicated, may hold values from 0.001 to 0.02
- send_rows: int32 [16384, 32], P('dom'), may hold values from 0 to 8191
- send_count: int32 [16384], P('dom'), may hold values from 16 to 32, as said below
- tiles: bfloat16 [8192, 8, 128, 128], P('dom'), as said below
- tile_col: int32 [8192, 8], P('dom'), may hold values from 0 to 95
- tile_count: int32 [8192], P('dom'), may hold values from 2 to 8, as said below
Outputs:
- log_scores: float32 [1048576, 172], P('dom')
Inputs may be any that keep to these rules, and one draw needn't show every extreme that they name: `send_count`: at most 32 slots are used from one partition to another; in every draw some partition receives 32 rows from every partition. `tile_count`: in every partition some row block uses all 8 slots. `tiles`: Nonnegative.
All inputs are finite; a program needn't handle non-finite values.
Results may differ from a plain program's by a relative error of at most 0.00085.
Values may be sent and summed in bfloat16 or wider, within the bound.
A program may use at most 128 MiB of HBM per device.

v0:
```python
import jax
import jax.numpy as jnp
from jax import lax
from jax.sharding import PartitionSpec as P

C = 172
B = 128
TPR = 8
SLOT = 32
STEPS = 3


MOMENTUM = 0.7
PROPAGATE = 0.9
LOG_FLOOR = 0.0001


def align_rows(class_values, ratio):
    scaled = class_values.astype(jnp.float32) * ratio
    row_total = jnp.sum(scaled, axis=-1, keepdims=True)
    return scaled / jnp.where(row_total > 0.0, row_total, 1.0)


def to_columns(row_major):
    return jnp.transpose(row_major.reshape(-1, B, C), (0, 2, 1))


def to_rows(column_major):
    return jnp.transpose(column_major, (0, 2, 1)).reshape(-1, C)


def on_device(
    features,
    teacher_w,
    teacher_b,
    ema_prior,
    target_prior,
    send_rows,
    send_count,
    tiles,
    tile_col,
    tile_count,
):
    row_count = features.shape[0]
    node_total = row_count * lax.axis_size("dom")
    logits = jnp.dot(features, teacher_w, preferred_element_type=jnp.float32) + teacher_b
    class_probs = jax.nn.softmax(logits, axis=-1).astype(jnp.bfloat16)
    local_marginal = jnp.sum(class_probs, axis=0, dtype=jnp.float32)
    slot_live = jnp.arange(SLOT)[None, :] < send_count[:, None]
    tile_used = jnp.arange(TPR)[None, :] < tile_count[:, None]
    live_tiles = jnp.where(tile_used[:, :, None, None], tiles, jnp.zeros((), jnp.bfloat16))

    def send_boundary(label_rows):
        picked = label_rows[send_rows]
        picked = jnp.where(slot_live[:, :, None], picked, jnp.zeros((), jnp.bfloat16))
        received = lax.all_to_all(picked, "dom", split_axis=0, concat_axis=0, tiled=True)
        return received.reshape(-1, C)

    marginal_sum = lax.psum(local_marginal, "dom")
    marginal = MOMENTUM * ema_prior + (1.0 - MOMENTUM) * marginal_sum / node_total
    ratio = target_prior / marginal
    seed_labels = align_rows(class_probs, ratio)
    far_labels = send_boundary(seed_labels.astype(jnp.bfloat16))
    seed_columns = to_columns(seed_labels)
    current_columns = seed_columns
    label_columns = seed_columns.astype(jnp.bfloat16)
    label_rows = seed_labels.astype(jnp.bfloat16)
    for iteration in range(STEPS):
        if iteration > 0:
            far_labels = send_boundary(label_rows)
        blocks = jnp.concatenate([label_columns, to_columns(far_labels)], axis=0)
        picked_blocks = blocks[tile_col]
        mixed_sum = jnp.einsum(
            "rtij,rtcj->rci", live_tiles, picked_blocks, preferred_element_type=jnp.float32
        )
        current_columns = PROPAGATE * mixed_sum + (1.0 - PROPAGATE) * seed_columns
        label_columns = current_columns.astype(jnp.bfloat16)
        if iteration + 1 < STEPS:
            label_rows = to_rows(label_columns)
    return jnp.log(to_rows(current_columns) + LOG_FLOOR)


def solution(mesh):
    placed = (
        P("dom", None),
        P(),
        P(),
        P(),
        P(),
        P("dom", None),
        P("dom"),
        P("dom", None, None, None),
        P("dom", None),
        P("dom"),
    )
    return jax.shard_map(
        on_device, mesh=mesh, in_specs=placed, out_specs=P("dom", None), check_vma=False
    )
```

profile of v0, /device:TPU:1, one launch (start us, length us, event | category | flops | bytes accessed | tf_op | source)
XLA Modules:
  0.0 417.7 jit_solution(1449636996899969195)
XLA Ops:
  0.0 0.9 iota_compare_fusion
  0.9 0.7 compare_select_fusion.1
  1.6 0.1 copy.49
  1.7 0.1 reshape.72
  1.8 1.7 fusion.26
  3.6 0.8 fusion.17
  4.4 0.0 copy-start.11
  4.4 0.0 copy-start.12
  4.4 3.2 convert_reduce_fusion
  7.6 68.6 %psum.7 = f32[172]{0:T(256)S(1)} all-reduce(f32[172]{0:T(256)S(1)} %get-tuple-element.5), channel_id=1, replica_groups=mesh['dom'=128] {'dom'}, use_global_device_ids=true, to_apply=%region_3.4 | all-reduce | flops 172 | bytes 1376 | tf_op jit(solution)/shard_map/psum | solution.py:59
  76.3 2.5 fusion.7
  78.8 6.5 %fusion.18 = (f32[8192,172]{0,1:T(8,128)}, bf16[8192,172]{0,1:T(8,128)(2,1)}) fusion(bf16[8192,172]{0,1:T(8,128)(2,1)} %get-tuple-element.6, f32[8192]{0:T(1024)S(1)} %compare_select_fusion, f32[172]{0:T(256)S(1)} %add_divide_fusion), kind=kLoop, calls=%fused_computation.40 | loop fusion | flops 7045120 | bytes 11305648 | tf_op jit(solution)/shard_map/mul | solution.py:76
  85.3 5.8 %copy.50 = bf16[8192,172]{1,0:T(8,128)(2,1)} copy(bf16[8192,172]{0,1:T(8,128)(2,1)} %get-tuple-element.8) | data formatting | bytes 5636096 | tf_op jit(solution)/shard_map/convert_element_type | solution.py:66
  91.1 15.7 %gather_fusion = bf16[4096,172]{1,0:T(8,128)(2,1)S(1)} fusion(bf16[8192,172]{1,0:T(8,128)(2,1)} %copy.50, s32[4096]{0:T(1024)S(1)} %broadcast_clamp_fusion), kind=kCustom, calls=%fused_computation | custom fusion | bytes 2834432 | tf_op jit(solution)/shard_map/gather | solution.py:54
  106.8 0.0 copy-start.10
  106.8 1.8 broadcast_select_fusion.12
  108.6 5.0 %all-to-all-start = ((bf16[128,32,172]{2,1,0:T(8,128)(2,1)}), bf16[128,32,172]{2,1,0:T(8,128)(2,1)S(1)}, u32[]{:S(2)}, u32[]{:S(2)}) async-start(bf16[128,32,172]{2,1,0:T(8,128)(2,1)} %broadcast_select_fusion.12), calls=%async_computation | async-start | bytes 4194304 | tf_op jit(solution)/shard_map/all_to_all | solution.py:56
  113.6 0.1 copy.52
  113.7 0.1 reshape.80
  113.8 6.4 %copy.68 = f32[22,8,64,128]{3,2,1,0:T(8,128)} copy(f32[22,8,64,128]{3,1,2,0:T(8,128)} %bitcast.95) | data formatting | bytes 11534336
  120.1 0.0 copy-done.2
  120.1 0.8 copy.67
  120.9 0.0 copy-start.13
  120.9 0.6 slice_bitcast_fusion
  121.6 3.4 copy.84
  125.0 0.6 pad_clamp_fusion
  125.6 0.7 iota_compare_fusion.1
  126.2 17.7 %all-to-all-done = bf16[128,32,172]{2,1,0:T(8,128)(2,1)S(1)} async-done(((bf16[128,32,172]{2,1,0:T(8,128)(2,1)}), bf16[128,32,172]{2,1,0:T(8,128)(2,1)S(1)}, u32[]{:S(2)}, u32[]{:S(2)}) %all-to-all-start) | async-done | bytes 1409056 | tf_op jit(solution)/shard_map/all_to_all | solution.py:56
  144.0 2.6 copy.51
  146.6 4.3 %pad_maximum_fusion = bf16[96,172,128]{2,1,0:T(8,128)(2,1)} fusion(bf16[32,172,128]{2,1,0:T(8,128)(2,1)S(1)} %bitcast.105, bf16[64,172,128]{2,1,0:T(8,128)(2,1)} %bitcast.97), kind=kLoop, calls=%fused_computation.37 | loop fusion | flops 2113536 | bytes 8454144 | tf_op jit(solution)/shard_map/concatenate | solution.py:71
  150.9 18.0 %gather_fusion.1 = bf16[512,172,128]{2,1,0:T(8,128)(2,1)} fusion(bf16[96,172,128]{2,1,0:T(8,128)(2,1)} %pad_maximum_fusion, s32[1024]{0:T(1024)S(1)} %copy-done.5), kind=kCustom, calls=%fused_computation.1 | custom fusion | bytes 45090816 | tf_op jit(solution)/shard_map/gather | solution.py:72
  168.8 14.9 %fusion.20 = f32[64,172,128]{2,1,0:T(8,128)S(1)} fusion(bf16[64,8,172,128]{3,2,1,0:T(8,128)(2,1)} %bitcast.93, bf16[64,8,128,128]{3,2,1,0:T(8,128)(2,1)} %param.17, pred[64,8]{1,0:T(8,128)(4,1)S(1)} %copy-done.9), kind=kOutput, calls=%fused_computation.44 | convolution fusion | flops 2894069760 | bytes 44958208 | tf_op jit(solution)/shard_map/rtij,rtcj->rci/dot_general | solution.py:73
  183.7 0.0 copy-start.4
  183.8 2.5 copy-done.4
  186.3 7.1 %fusion.12 = bf16[64,128,172]{1,0,2:T(8,128)(2,1)} fusion(f32[64,172,128]{2,1,0:T(8,128)S(1)} %fusion.20, f32[176,64,128]{2,1,0:T(8,128)} %bitcast.84), kind=kLoop, calls=%fused_computation.28 | loop fusion | flops 4227072 | bytes 14090240 | tf_op jit(solution)/shard_map/convert_element_type | solution.py:77
  193.3 6.8 %copy.65 = bf16[64,128,172]{2,1,0:T(8,128)(2,1)} copy(bf16[64,128,172]{1,0,2:T(8,128)(2,1)} %fusion.12) | data formatting | bytes 5636096 | tf_op jit(solution)/shard_map/reshape | solution.py:29
  200.1 15.7 %gather_fusion.2 = bf16[4096,172]{1,0:T(8,128)(2,1)S(1)} fusion(bf16[8192,172]{1,0:T(8,128)(2,1)} %bitcast.90, s32[4096]{0:T(1024)S(1)} %broadcast_clamp_fusion), kind=kCustom, calls=%fused_computation.2 | custom fusion | bytes 2834432 | tf_op jit(solution)/shard_map/gather | solution.py:54
  215.9 1.7 broadcast_select_fusion.11
  217.6 4.9 %all-to-all-start.1 = ((bf16[128,32,172]{2,1,0:T(8,128)(2,1)}), bf16[128,32,172]{2,1,0:T(8,128)(2,1)S(1)}, u32[]{:S(2)}, u32[]{:S(2)}) async-start(bf16[128,32,172]{2,1,0:T(8,128)(2,1)} %broadcast_select_fusion.11), calls=%async_computation.1 | async-start | bytes 4194304 | tf_op jit(solution)/shard_map/all_to_all | solution.py:56
  222.4 8.0 %fusion.10 = bf16[64,172,128]{2,0,1:T(8,128)(2,1)} fusion(f32[64,172,128]{2,1,0:T(8,128)} %copy-done.4, f32[176,64,128]{2,1,0:T(8,128)} %bitcast.85), kind=kLoop, calls=%fused_computation.26 | loop fusion | flops 4227072 | bytes 14090240 | tf_op jit(solution)/shard_map/convert_element_type | solution.py:77
  230.5 22.5 %all-to-all-done.1 = bf16[128,32,172]{2,1,0:T(8,128)(2,1)S(1)} async-done(((bf16[128,32,172]{2,1,0:T(8,128)(2,1)}), bf16[128,32,172]{2,1,0:T(8,128)(2,1)S(1)}, u32[]{:S(2)}, u32[]{:S(2)}) %all-to-all-start.1) | async-done | bytes 1409056 | tf_op jit(solution)/shard_map/all_to_all | solution.py:56
  253.0 1.5 copy.55
  254.5 2.6 pad_maximum_fusion.1
  257.1 3.7 copy.56
  260.8 18.0 %gather_fusion.3 = bf16[512,172,128]{2,1,0:T(8,128)(2,1)} fusion(bf16[96,172,128]{2,1,0:T(8,128)(2,1)} %copy.56, s32[1024]{0:T(1024)S(1)} %copy-done.6), kind=kCustom, calls=%fused_computation.3 | custom fusion | bytes 45090816 | tf_op jit(solution)/shard_map/gather | solution.py:72
  278.8 15.1 %fusion.21 = f32[64,172,128]{2,1,0:T(8,128)S(1)} fusion(bf16[64,8,172,128]{3,2,1,0:T(8,128)(2,1)} %bitcast.94, bf16[64,8,128,128]{3,2,1,0:T(8,128)(2,1)} %param.17, pred[64,8]{1,0:T(8,128)(4,1)S(1)} %copy-done.9), kind=kOutput, calls=%fused_computation.45 | convolution fusion | flops 2894069760 | bytes 44958208 | tf_op jit(solution)/shard_map/rtij,rtcj->rci/dot_general | solution.py:73
  293.8 0.0 copy-start.3
  293.9 2.5 copy-done.3
  296.4 7.1 %fusion.13 = bf16[64,128,172]{1,0,2:T(8,128)(2,1)} fusion(f32[64,172,128]{2,1,0:T(8,128)S(1)} %fusion.21, f32[176,64,128]{2,1,0:T(8,128)} %bitcast.86), kind=kLoop, calls=%fused_computation.29 | loop fusion | flops 4227072 | bytes 14090240 | tf_op jit(solution)/shard_map/convert_element_type | solution.py:77
  303.5 6.8 %copy.66 = bf16[64,128,172]{2,1,0:T(8,128)(2,1)} copy(bf16[64,128,172]{1,0,2:T(8,128)(2,1)} %fusion.13) | data formatting | bytes 5636096 | tf_op jit(solution)/shard_map/reshape | solution.py:29
  310.2 15.7 %gather_fusion.4 = bf16[4096,172]{1,0:T(8,128)(2,1)S(1)} fusion(bf16[8192,172]{1,0:T(8,128)(2,1)} %bitcast.89, s32[4096]{0:T(1024)S(1)} %broadcast_clamp_fusion), kind=kCustom, calls=%fused_computation.4 | custom fusion | bytes 2834432 | tf_op jit(solution)/shard_map/gather | solution.py:54
  326.0 1.7 broadcast_select_fusion.10
  327.7 4.3 %all-to-all-start.2 = ((bf16[128,32,172]{2,1,0:T(8,128)(2,1)}), bf16[128,32,172]{2,1,0:T(8,128)(2,1)S(1)}, u32[]{:S(2)}, u32[]{:S(2)}) async-start(bf16[128,32,172]{2,1,0:T(8,128)(2,1)} %broadcast_select_fusion.10), calls=%async_computation.2 | async-start | bytes 4194304 | tf_op jit(solution)/shard_map/all_to_all | solution.py:56
  332.0 8.0 %fusion.11 = bf16[64,172,128]{2,0,1:T(8,128)(2,1)} fusion(f32[64,172,128]{2,1,0:T(8,128)} %copy-done.3, f32[176,64,128]{2,1,0:T(8,128)} %bitcast.87), kind=kLoop, calls=%fused_computation.27 | loop fusion | flops 4227072 | bytes 14090240 | tf_op jit(solution)/shard_map/convert_element_type | solution.py:77
  340.0 22.6 %all-to-all-done.2 = bf16[128,32,172]{2,1,0:T(8,128)(2,1)S(1)} async-done(((bf16[128,32,172]{2,1,0:T(8,128)(2,1)}), bf16[128,32,172]{2,1,0:T(8,128)(2,1)S(1)}, u32[]{:S(2)}, u32[]{:S(2)}) %all-to-all-start.2) | async-done | bytes 1409056 | tf_op jit(solution)/shard_map/all_to_all | solution.py:56
  362.7 1.5 copy.59
  364.1 2.6 pad_maximum_fusion.2
  366.8 3.7 copy.60
  370.5 17.9 %gather_fusion.5 = bf16[512,172,128]{2,1,0:T(8,128)(2,1)} fusion(bf16[96,172,128]{2,1,0:T(8,128)(2,1)} %copy.60, s32[1024]{0:T(1024)S(1)} %copy-done.6), kind=kCustom, calls=%fused_computation.5 | custom fusion | bytes 45090816 | tf_op jit(solution)/shard_map/gather | solution.py:72
  388.4 15.2 %fusion.22 = f32[64,128,172]{1,2,0:T(8,128)S(1)} fusion(bf16[64,8,172,128]{3,2,1,0:T(8,128)(2,1)} %bitcast.92, bf16[64,8,128,128]{3,2,1,0:T(8,128)(2,1)} %param.17, pred[64,8]{1,0:T(8,128)(4,1)S(1)} %copy-done.9), kind=kOutput, calls=%fused_computation.46 | convolution fusion | flops 2894069760 | bytes 44958208 | tf_op jit(solution)/shard_map/rtij,rtcj->rci/dot_general | solution.py:73
  403.6 5.7 %fusion.16 = f32[172,64,128]{2,1,0:T(8,128)S(1)} fusion(f32[64,128,172]{1,2,0:T(8,128)S(1)} %fusion.22, f32[176,64,128]{2,1,0:T(8,128)} %bitcast.88), kind=kLoop, calls=%fused_computation.32 | loop fusion | flops 4227072 | bytes 16908288
  409.3 0.7 pad.12
  410.0 0.0 copy-start.1
  410.0 7.5 %copy.69 = f32[22,8,64,128]{3,1,2,0:T(8,128)} copy(f32[22,8,64,128]{3,2,1,0:T(8,128)S(1)} %bitcast.96) | data formatting | bytes 11534336
  (22 shorter events, 0.1 us)
Async XLA Ops:
  0.0 1.8 copy-start
  0.9 105.9 %copy-start.7 = (pred[128,32]{1,0:T(8,128)(4,1)}, pred[128,32]{1,0:T(8,128)(4,1)S(1)}, u32[]{:S(2)}) copy-start(pred[128,32]{1,0:T(8,128)(4,1)S(1)} %iota_compare_fusion) | copy-start | bytes 12292
  4.4 71.9 %copy-start.11 = (f32[172]{0:T(256)S(1)}, f32[172]{0:T(256)}, u32[]{:S(2)}) copy-start(f32[172]{0:T(256)} %param.14) | copy-start | bytes 2068
  4.4 71.9 %copy-start.12 = (f32[172]{0:T(256)S(1)}, f32[172]{0:T(256)}, u32[]{:S(2)}) copy-start(f32[172]{0:T(256)} %param.13) | copy-start | bytes 2068
  106.8 6.8 %copy-start.10 = (s32[64,8]{0,1:T(8,128)S(1)}, s32[64,8]{0,1:T(8,128)}, u32[]{:S(2)}) copy-start(s32[64,8]{0,1:T(8,128)} %param.18) | copy-start | bytes 6148
  108.6 35.4 %all-to-all-start = ((bf16[128,32,172]{2,1,0:T(8,128)(2,1)}), bf16[128,32,172]{2,1,0:T(8,128)(2,1)S(1)}, u32[]{:S(2)}, u32[]{:S(2)}) async-start(bf16[128,32,172]{2,1,0:T(8,128)(2,1)} %broadcast_select_fusion.12), calls=%async_computation | async-start | bytes 4194304 | tf_op jit(solution)/shard_map/all_to_all | solution.py:56
  113.8 6.4 %copy-start.2 = (bf16[8192,172]{0,1:T(8,128)(2,1)S(1)}, bf16[8192,172]{0,1:T(8,128)(2,1)}, u32[]{:S(2)}) copy-start(bf16[8192,172]{0,1:T(8,128)(2,1)} %get-tuple-element.8) | copy-start | bytes 8454148
  120.9 4.6 %copy-start.13 = (s32[64]{0:T(128)S(1)}, s32[64]{0:T(128)}, u32[]{:S(2)}) copy-start(s32[64]{0:T(128)} %param.19) | copy-start | bytes 772
  146.6 4.3 %copy-start.5 = (s32[1024]{0:T(1024)S(1)}, s32[1024]{0:T(1024)}, u32[]{:S(2)}) copy-start(s32[1024]{0:T(1024)} %pad_clamp_fusion) | copy-start | bytes 12292
  150.9 18.0 %copy-start.9 = (pred[64,8]{1,0:T(8,128)(4,1)S(1)}, pred[64,8]{1,0:T(8,128)(4,1)}, u32[]{:S(2)}) copy-start(pred[64,8]{1,0:T(8,128)(4,1)} %iota_compare_fusion.1) | copy-start | bytes 1540
  183.7 2.5 copy-start.4
  200.1 15.7 %copy-start.8 = (pred[128,32]{1,0:T(8,128)(4,1)S(1)}, pred[128,32]{1,0:T(8,128)(4,1)}, u32[]{:S(2)}) copy-start(pred[128,32]{1,0:T(8,128)(4,1)} %copy-done.7) | copy-start | bytes 12292
  217.6 35.4 %all-to-all-start.1 = ((bf16[128,32,172]{2,1,0:T(8,128)(2,1)}), bf16[128,32,172]{2,1,0:T(8,128)(2,1)S(1)}, u32[]{:S(2)}, u32[]{:S(2)}) async-start(bf16[128,32,172]{2,1,0:T(8,128)(2,1)} %broadcast_select_fusion.11), calls=%async_computation.1 | async-start | bytes 4194304 | tf_op jit(solution)/shard_map/all_to_all | solution.py:56
  257.1 3.7 copy-start.6
  293.8 2.5 copy-start.3
  327.7 35.0 %all-to-all-start.2 = ((bf16[128,32,172]{2,1,0:T(8,128)(2,1)}), bf16[128,32,172]{2,1,0:T(8,128)(2,1)S(1)}, u32[]{:S(2)}, u32[]{:S(2)}) async-start(bf16[128,32,172]{2,1,0:T(8,128)(2,1)} %broadcast_select_fusion.10), calls=%async_computation.2 | async-start | bytes 4194304 | tf_op jit(solution)/shard_map/all_to_all | solution.py:56
  410.0 7.5 %copy-start.1 = (bf16[8192,128]{1,0:T(8,128)(2,1)S(1)}, bf16[8192,128]{1,0:T(8,128)(2,1)}, u32[]{:S(2)}) copy-start(bf16[8192,128]{1,0:T(8,128)(2,1)} %param.10) | copy-start | bytes 6291460
where the time goes:
time: 425 us; the launch traced here: 418 us
  local copies, waits for them, and re-layouts  158 us (37%)
  blocking collectives  68.6 us (16%)
  other arithmetic  66.5 us (16%)
  waiting for transfers between devices  62.9 us (15%)
  matrix products  46.9 us (11%)
  starting transfers between devices  14.2 us (3%)
    psum x1, blocking collectives, on_device(): marginal_sum = lax.psum(local_marginal, 'dom')  68.6 us
    all_to_all x3, waiting for transfers between devices, send_boundary(): lax.all_to_all(picked, 'dom', split_axis=0, concat_axis=0, tiled=True)  62.9 us
    gather x3, local copies, waits for them, and re-layouts, on_device(): picked_blocks = blocks[tile_col]  53.9 us
    gather x3, local copies, waits for them, and re-layouts, send_boundary(): picked = label_rows[send_rows]  47.2 us
    dot_general x3, matrix products, on_device(): jnp.einsum('rtij,rtcj->rci', live_tiles, picked_blocks, preferred_element...  45.1 us
    convert_element_type x4, other arithmetic, on_device(): label_columns = current_columns.astype(jnp.bfloat16)  30.2 us
    unnamed x32, local copies, waits for them, and re-layouts  20.4 us
    all_to_all x3, starting transfers between devices, send_boundary(): lax.all_to_all(picked, 'dom', split_axis=0, concat_axis=0, tiled=True)  14.2 us
  transfers between devices with their start and end apart: 3, of which 3 were waited for; matrix products, arithmetic and copies ran while one was open for 7% of the time, Pallas kernels for 0%

commit v1 on v0

v1 whole, which is shorter than its diff:
```python
import functools

import jax
import jax.numpy as jnp
from jax import lax
from jax.experimental import pallas as pl
from jax.experimental.pallas import tpu as pltpu
from jax.sharding import PartitionSpec as P

F = 128
C = 172
CP = 256
B = 128
RB = 64
TPR = 8
SLOT = 32
PACK = 48
HB = 32
ROWS = 8192
N = 128
NODES = ROWS * N

MOMENTUM = 0.7
PROPAGATE = 0.9
LOG_FLOOR = 0.0001
DEAD = 32768.0
LOW = -1e30
MESH = pl.DeviceIdType.MESH
MIX = 37
GROUP = 16
F32 = jnp.float32
BF16 = jnp.bfloat16


def full_vmem():
    return pl.BlockSpec(memory_space=pltpu.VMEM)


def full_smem():
    return pl.BlockSpec(memory_space=pltpu.SMEM)


def greet(me):
    barrier = pltpu.get_barrier_semaphore()

    def tell(k, carry):
        other = lax.rem(me + k, N)
        pl.semaphore_signal(barrier, inc=1, device_id=(other,), device_id_type=MESH)
        return carry

    lax.fori_loop(1, N, tell, 0)
    return barrier


def softmax_rows(feats, wt, bias):
    logits = lax.dot_general(feats, wt, (((1,), (1,)), ((), ())), preferred_element_type=F32) + bias
    top = jnp.max(logits, axis=-1, keepdims=True)
    e = jnp.exp(logits - top)
    return (e / jnp.sum(e, axis=-1, keepdims=True)).astype(BF16)


def fill_teacher(wt_ref, b_ref, wpad, bpad):
    wpad[...] = jnp.zeros_like(wpad)
    wpad[pl.ds(0, C), :] = wt_ref[...].astype(F32)
    bpad[...] = jnp.full(bpad.shape, LOW, F32)
    bpad[:, pl.ds(0, C)] = b_ref[...]


def teacher_kernel(
    rows_ref, cnt_ref, feat_ref, wt_ref, b_ref,
    probs_ref, recv_ref, total_ref,
    feat32, stage, sendbuf, wpad, bpad, part1, part2,
    send_sem, recv_sem, send1, recv1, send2, recv2,
):
    me = lax.axis_index("dom")
    barrier = greet(me)

    def widen(k, carry):
        at = pl.multiple_of(k * 256, 256)
        feat32[pl.ds(at, 256), :] = feat_ref[pl.ds(at, 256), :].astype(F32)
        return carry

    lax.fori_loop(0, ROWS // 256, widen, 0)
    fill_teacher(wt_ref, b_ref, wpad, bpad)

    def gather(dest):
        for j in range(SLOT):
            stage[pl.ds(j, 1), :] = feat32[pl.ds(rows_ref[j, dest], 1), :]
        live = lax.broadcasted_iota(jnp.int32, (SLOT, F), 0) < cnt_ref[dest]
        return jnp.where(live, stage[...], DEAD).astype(BF16)

    recv_ref[pl.ds(me, 1)] = gather(me)[None]
    pl.semaphore_wait(barrier, N - 1)

    def send(k, carry):
        dest = lax.rem(me + lax.rem(k * MIX, N), N)
        sendbuf[pl.ds(k, 1)] = gather(dest)[None]
        pltpu.make_async_remote_copy(
            src_ref=sendbuf.at[k], dst_ref=recv_ref.at[me], send_sem=send_sem, recv_sem=recv_sem,
            device_id=(dest,), device_id_type=MESH,
        ).start()
        return carry

    lax.fori_loop(1, N, send, 0)

    wt = wpad[...].astype(BF16)
    bias = bpad[...]

    def local(k, acc):
        at = pl.multiple_of(k * 256, 256)
        p = softmax_rows(feat_ref[pl.ds(at, 256), :], wt, bias)
        probs_ref[pl.ds(at, 256), :] = p
        return acc + jnp.sum(p.astype(F32).reshape(32, 8, CP), axis=0)

    acc = lax.fori_loop(0, ROWS // 256, local, jnp.zeros((8, CP), F32))

    group = me // GROUP
    place = lax.rem(me, GROUP)
    part1[pl.ds(place, 1)] = acc[None]

    def send_near(k, carry):
        other = group * GROUP + lax.rem(place + k, GROUP)
        pltpu.make_async_remote_copy(
            src_ref=part1.at[place], dst_ref=part1.at[place], send_sem=send1, recv_sem=recv1,
            device_id=(other,), device_id_type=MESH,
        ).start()
        return carry

    lax.fori_loop(1, GROUP, send_near, 0)
    near = pltpu.make_async_remote_copy(
        src_ref=part1.at[pl.ds(0, GROUP - 1)], dst_ref=part1.at[pl.ds(0, GROUP - 1)], send_sem=send1, recv_sem=recv1,
        device_id=(lax.rem(me + 1, N),), device_id_type=MESH,
    )
    near.wait_recv()
    part2[pl.ds(group, 1)] = jnp.sum(part1[...], axis=0)[None]

    groups = N // GROUP

    def send_far(k, carry):
        other = lax.rem(group + k, groups) * GROUP + place
        pltpu.make_async_remote_copy(
            src_ref=part2.at[group], dst_ref=part2.at[group], send_sem=send2, recv_sem=recv2,
            device_id=(other,), device_id_type=MESH,
        ).start()
        return carry

    lax.fori_loop(1, groups, send_far, 0)
    far = pltpu.make_async_remote_copy(
        src_ref=part2.at[pl.ds(0, groups - 1)], dst_ref=part2.at[pl.ds(0, groups - 1)], send_sem=send2, recv_sem=recv2,
        device_id=(lax.rem(me + 1, N),), device_id_type=MESH,
    )
    far.wait_recv()
    total_ref[...] = jnp.sum(part2[...], axis=0)
    near.wait_send()
    far.wait_send()
    bulk = pltpu.make_async_remote_copy(
        src_ref=sendbuf.at[pl.ds(0, N - 1)], dst_ref=recv_ref.at[pl.ds(0, N - 1)], send_sem=send_sem, recv_sem=recv_sem,
        device_id=(lax.rem(me + 1, N),), device_id_type=MESH,
    )
    bulk.wait_recv()
    bulk.wait_send()


def teacher(rows_t, counts, features, wt, bias):
    return pl.pallas_call(
        teacher_kernel,
        out_shape=(
            jax.ShapeDtypeStruct((ROWS, CP), BF16),
            jax.ShapeDtypeStruct((N, SLOT, F), BF16),
            jax.ShapeDtypeStruct((8, CP), F32),
        ),
        in_specs=[full_smem(), full_smem(), full_vmem(), full_vmem(), full_vmem()],
        out_specs=(full_vmem(), full_vmem(), full_vmem()),
        scratch_shapes=[
            pltpu.VMEM((ROWS, F), F32),
            pltpu.VMEM((SLOT, F), F32),
            pltpu.VMEM((N, SLOT, F), BF16),
            pltpu.VMEM((CP, F), F32),
            pltpu.VMEM((1, CP), F32),
            pltpu.VMEM((GROUP, 8, CP), F32),
            pltpu.VMEM((N // GROUP, 8, CP), F32),
        ] + [pltpu.SemaphoreType.DMA] * 6,
        compiler_params=pltpu.CompilerParams(collective_id=0, has_side_effects=True, vmem_limit_bytes=40 * 2**20),
        cost_estimate=pl.CostEstimate(flops=2 * ROWS * F * CP, bytes_accessed=8 * 2**20, transcendentals=ROWS * CP),
        name="teacher",
    )(rows_t, counts, features, wt, bias)


def exchange_kernel(rows_ref, cnt_ref, labels_ref, recv_ref, wide, stage, sendbuf, send_sem, recv_sem):
    me = lax.axis_index("dom")
    barrier = greet(me)

    def widen(k, carry):
        at = pl.multiple_of(k * 128, 128)
        wide[pl.ds(at, 128), :] = labels_ref[pl.ds(at, 128), :].astype(F32)
        return carry

    lax.fori_loop(0, ROWS // 128, widen, 0)

    def gather(dest):
        for j in range(SLOT):
            stage[pl.ds(j, 1), :] = wide[pl.ds(rows_ref[j, dest], 1), :]
        live = lax.broadcasted_iota(jnp.int32, (SLOT, CP), 0) < cnt_ref[dest]
        rows = jnp.where(live, stage[...], 0.0)
        high = rows[:, F:]
        lane = lax.broadcasted_iota(jnp.int32, (SLOT // 2, F), 1)
        high = jnp.where(lane < F // 2, high[: SLOT // 2], pltpu.roll(high[SLOT // 2 :], F // 2, 1))
        return jnp.concatenate([rows[:, :F], high], axis=0).astype(BF16)

    recv_ref[pl.ds(me, 1)] = gather(me)[None]
    pl.semaphore_wait(barrier, N - 1)

    def send(k, carry):
        dest = lax.rem(me + lax.rem(k * MIX, N), N)
        sendbuf[pl.ds(k, 1)] = gather(dest)[None]
        pltpu.make_async_remote_copy(
            src_ref=sendbuf.at[k], dst_ref=recv_ref.at[me], send_sem=send_sem, recv_sem=recv_sem,
            device_id=(dest,), device_id_type=MESH,
        ).start()
        return carry

    lax.fori_loop(1, N, send, 0)
    bulk = pltpu.make_async_remote_copy(
        src_ref=sendbuf.at[pl.ds(0, N - 1)], dst_ref=recv_ref.at[pl.ds(0, N - 1)], send_sem=send_sem, recv_sem=recv_sem,
        device_id=(lax.rem(me + 1, N),), device_id_type=MESH,
    )
    bulk.wait_recv()
    bulk.wait_send()


def exchange(rows_t, counts, labels, number):
    return pl.pallas_call(
        exchange_kernel,
        out_shape=jax.ShapeDtypeStruct((N, PACK, F), BF16),
        in_specs=[full_smem(), full_smem(), full_vmem()],
        out_specs=full_vmem(),
        scratch_shapes=[
            pltpu.VMEM((ROWS, CP), F32),
            pltpu.VMEM((SLOT, CP), F32),
            pltpu.VMEM((N, PACK, F), BF16),
        ] + [pltpu.SemaphoreType.DMA] * 2,
        compiler_params=pltpu.CompilerParams(collective_id=number, has_side_effects=True, vmem_limit_bytes=40 * 2**20),
        cost_estimate=pl.CostEstimate(flops=0, bytes_accessed=8 * 2**20, transcendentals=0),
        name="exchange",
    )(rows_t, counts, labels)


PER = 4


def products(r, tiles_ref, local_r, col_ref, count_ref, labels, acc_ref):
    count = count_ref[r]
    cols = [jnp.where(t < count, col_ref[t, r], RB + HB) for t in range(TPR)]
    for pairs in range(1, TPR // 2 + 1):
        here = (count + 1) // 2 == pairs if pairs > 1 else count <= 2

        @pl.when(here)
        def _():
            lhs = jnp.concatenate([tiles_ref[local_r, t] for t in range(2 * pairs)], axis=1)
            rhs = jnp.concatenate([labels[cols[t]] for t in range(2 * pairs)], axis=0)
            acc_ref[...] = jnp.dot(lhs, rhs, preferred_element_type=F32)


def first_kernel(
    count_ref, col_ref, tiles_ref, probs_hbm, feats_ref, total_ref, ema_ref, target_ref, wt_ref, b_ref,
    seed_ref, out_ref,
    labels, feats, acc_ref, wpad, bpad, ratio_ref, ema, target, sem,
):
    step = pl.program_id(0)

    @pl.when(step == 0)
    def _():
        copy = pltpu.make_async_copy(probs_hbm, labels.at[pl.ds(0, RB)], sem)
        copy.start()
        fill_teacher(wt_ref, b_ref, wpad, bpad)
        ema[...] = jnp.full(ema.shape, 1.0, F32)
        ema[:, pl.ds(0, C)] = ema_ref[...]
        target[...] = jnp.zeros_like(target)
        target[:, pl.ds(0, C)] = target_ref[...]
        total = jnp.sum(total_ref[...], axis=0, keepdims=True)
        marginal = MOMENTUM * ema[...] + (1.0 - MOMENTUM) * total / NODES
        ratio_ref[...] = target[...] / marginal
        labels[pl.ds(RB + HB, 1)] = jnp.zeros((1, B, CP), BF16)
        wt = wpad[...].astype(BF16)
        bias = bpad[...]
        ratio = ratio_ref[...]

        def align(p):
            scaled = p.astype(F32) * ratio
            row_total = jnp.sum(scaled, axis=-1, keepdims=True)
            return scaled / jnp.where(row_total > 0.0, row_total, 1.0)

        def far(h, carry):
            f = feats_ref[pl.ds(pl.multiple_of(h * B, B), B), :]
            live = jnp.broadcast_to(f[:, :1].astype(F32) < DEAD / 2, (B, CP))
            p = softmax_rows(f, wt, bias)
            labels[pl.ds(RB + h, 1)] = jnp.where(live, align(p), 0.0).astype(BF16)[None]
            return carry

        lax.fori_loop(0, HB, far, 0)
        copy.wait()

        def near(r, carry):
            labels[pl.ds(r, 1)] = align(labels[r]).astype(BF16)[None]
            return carry

        lax.fori_loop(0, RB, near, 0)

    def block(i, carry):
        r = step * PER + i
        products(r, tiles_ref, i, col_ref, count_ref, labels, acc_ref)
        seed = labels[r]
        seed_ref[pl.ds(i, 1)] = seed[None]
        out_ref[pl.ds(i, 1)] = (PROPAGATE * acc_ref[...] + (1.0 - PROPAGATE) * seed.astype(F32)).astype(BF16)[None]
        return carry

    lax.fori_loop(0, PER, block, 0)


def later_kernel(last, count_ref, col_ref, tiles_ref, labels_hbm, far_ref, seed_ref, out_ref, labels, acc_ref, sem):
    step = pl.program_id(0)

    @pl.when(step == 0)
    def _():
        copy = pltpu.make_async_copy(labels_hbm, labels.at[pl.ds(0, RB)], sem)
        copy.start()
        labels[pl.ds(RB + HB, 1)] = jnp.zeros((1, B, CP), BF16)

        def far(h, carry):
            lane = lax.broadcasted_iota(jnp.int32, (SLOT // 2, F), 1)
            for s in range(B // SLOT):
                packed = far_ref[h * (B // SLOT) + s].astype(F32)
                high = packed[SLOT:]
                other = pltpu.roll(high, F // 2, 1)
                high = jnp.concatenate([high, other], axis=0)
                lane = lax.broadcasted_iota(jnp.int32, (SLOT, F), 1)
                high = jnp.where(lane < F // 2, high, 0.0)
                rows = jnp.concatenate([packed[:SLOT], high], axis=1).astype(BF16)
                labels[pl.ds(RB + h, 1), pl.ds(s * SLOT, SLOT), :] = rows[None]
            return carry

        lax.fori_loop(0, HB, far, 0)
        copy.wait()

    def block(i, carry):
        r = step * PER + i
        products(r, tiles_ref, i, col_ref, count_ref, labels, acc_ref)
        current = PROPAGATE * acc_ref[...] + (1.0 - PROPAGATE) * seed_ref[i].astype(F32)
        if last:
            flipped = current.T[:C]
            out_ref[:, pl.ds(pl.multiple_of(i * B, B), B)] = jnp.log(flipped + LOG_FLOOR)
        else:
            out_ref[pl.ds(i, 1)] = current.astype(BF16)[None]
        return carry

    lax.fori_loop(0, PER, block, 0)


def tile_spec():
    return pl.BlockSpec((PER, TPR, B, B), lambda i: (i, 0, 0, 0))


def label_spec():
    return pl.BlockSpec((PER, B, CP), lambda i: (i, 0, 0))


PRODUCT_COST = pl.CostEstimate(flops=2 * RB * TPR * B * B * CP, bytes_accessed=28 * 2**20, transcendentals=0)


def first_step(counts, cols_t, tiles, probs, feats, total, ema, target, wt, bias):
    shape = jax.ShapeDtypeStruct((RB, B, CP), BF16)
    return pl.pallas_call(
        first_kernel,
        grid=(RB // PER,),
        out_shape=(shape, shape),
        in_specs=[full_smem(), full_smem(), tile_spec(), pl.BlockSpec(memory_space=pl.ANY)] + [full_vmem()] * 6,
        out_specs=(label_spec(), label_spec()),
        scratch_shapes=[
            pltpu.VMEM((RB + HB + 1, B, CP), BF16),
            pltpu.VMEM((8, F), BF16),
            pltpu.VMEM((B, CP), F32),
            pltpu.VMEM((CP, F), F32),
            pltpu.VMEM((1, CP), F32),
            pltpu.VMEM((1, CP), F32),
            pltpu.VMEM((1, CP), F32),
            pltpu.VMEM((1, CP), F32),
            pltpu.SemaphoreType.DMA,
        ],
        compiler_params=pltpu.CompilerParams(vmem_limit_bytes=40 * 2**20),
        cost_estimate=PRODUCT_COST,
        name="first_step",
    )(counts, cols_t, tiles, probs.reshape(RB, B, CP), feats.reshape(HB * B, F), total, ema, target, wt, bias)


def later_step(last, counts, cols_t, tiles, labels, far, seed):
    if last:
        shape = jax.ShapeDtypeStruct((C, ROWS), F32)
        spec = pl.BlockSpec((C, PER * B), lambda i: (0, i))
    else:
        shape = jax.ShapeDtypeStruct((RB, B, CP), BF16)
        spec = label_spec()
    return pl.pallas_call(
        functools.partial(later_kernel, last),
        grid=(RB // PER,),
        out_shape=shape,
        in_specs=[full_smem(), full_smem(), tile_spec(), pl.BlockSpec(memory_space=pl.ANY), full_vmem(), label_spec()],
        out_specs=spec,
        scratch_shapes=[
            pltpu.VMEM((RB + HB + 1, B, CP), BF16),
            pltpu.VMEM((B, CP), F32),
            pltpu.SemaphoreType.DMA,
        ],
        compiler_params=pltpu.CompilerParams(vmem_limit_bytes=40 * 2**20),
        cost_estimate=PRODUCT_COST,
        name="last_step" if last else "later_step",
    )(counts, cols_t, tiles, labels, far, seed)


def on_device(
    features, teacher_w, teacher_b, ema_prior, target_prior, send_rows, send_count, tiles, tile_col, tile_count
):
    rows_t = send_rows.T
    cols_t = tile_col.T
    wt = teacher_w.T
    bias = teacher_b.reshape(1, C)
    probs, feats, total = teacher(rows_t, send_count, features, wt, bias)
    seed, labels = first_step(
        tile_count, cols_t, tiles, probs, feats, total, ema_prior.reshape(1, C), target_prior.reshape(1, C), wt, bias
    )
    far = exchange(rows_t, send_count, labels.reshape(ROWS, CP), 1)
    labels = later_step(False, tile_count, cols_t, tiles, labels, far, seed)
    far = exchange(rows_t, send_count, labels.reshape(ROWS, CP), 2)
    out_t = later_step(True, tile_count, cols_t, tiles, labels, far, seed)
    return out_t.T


def solution(mesh):
    placed = (
        P("dom", None), P(), P(), P(), P(), P("dom", None), P("dom"),
        P("dom", None, None, None), P("dom", None), P("dom"),
    )
    return jax.shard_map(on_device, mesh=mesh, in_specs=placed, out_specs=P("dom", None), check_vma=False)
```

time: 425 us -> 197 us (0.46); the launches traced: 418 us -> 195 us
  Pallas kernels: 0 us -> 187 us
  local copies, waits for them, and re-layouts: 158 us -> 7.8 us
  blocking collectives: 68.6 us -> 0 us
  other arithmetic: 66.5 us -> 0 us
  waiting for transfers between devices: 62.9 us -> 0 us
  matrix products: 46.9 us -> 0 us
  starting transfers between devices: 14.2 us -> 0 us
    pallas_call x0 -> x6, Pallas kernels: none -> 187 us  [the longest x2 57.1 us: exchange(): pl.pallas_call(exchange_kernel, out_shape=jax.ShapeDtypeStruct((N, PACK,...]
    gather x6 -> x0, local copies, waits for them, and re-layouts: 101 us -> none  [the longest x3 53.9 us: on_device(): picked_blocks = blocks[tile_col]]
    psum x1 -> x0, blocking collectives: 68.6 us -> none  [on_device(): marginal_sum = lax.psum(local_marginal, 'dom')]
    all_to_all x3 -> x0, waiting for transfers between devices: 62.9 us -> none  [send_boundary(): lax.all_to_all(picked, 'dom', split_axis=0, concat_axis=0, tiled=True)]
    dot_general x4 -> x0, matrix products: 46.9 us -> none  [the longest x3 45.1 us: on_device(): jnp.einsum('rtij,rtcj->rci', live_tiles, picked_blocks, preferred_element...]
    convert_element_type x4 -> x0, other arithmetic: 30.2 us -> none  [on_device(): label_columns = current_columns.astype(jnp.bfloat16)]
    all_to_all x3 -> x0, starting transfers between devices: 14.2 us -> none  [send_boundary(): lax.all_to_all(picked, 'dom', split_axis=0, concat_axis=0, tiled=True)]
    reshape x2 -> x0, local copies, waits for them, and re-layouts: 13.6 us -> none  [to_rows(): return jnp.transpose(column_major, (0, 2, 1)).reshape(-1, C)]
  transfers between devices with their start and end apart: 3 -> 0, of which waited for: 3 -> 0; matrix products, arithmetic and copies ran while one was open for 7% -> 0% of each run, Pallas kernels for 0% -> 0%
where the time goes in v1:
time: 197 us; the launch traced here: 195 us
  Pallas kernels  187 us (95%)
  local copies, waits for them, and re-layouts  7.8 us (4%)
    pallas_call x2, Pallas kernels, exchange(): pl.pallas_call(exchange_kernel, out_shape=jax.ShapeDtypeStruct((N, PACK,...  57.1 us
    pallas_call x2, Pallas kernels, later_step(): pl.pallas_call(functools.partial(later_kernel, last), grid=(RB // PER,),...  49.6 us
    pallas_call x1, Pallas kernels, first_step(): pl.pallas_call(first_kernel, grid=(RB // PER,), out_shape=(shape, shape),...  42.4 us
    pallas_call x1, Pallas kernels, teacher(): pl.pallas_call(teacher_kernel, out_shape=(jax.ShapeDtypeStruct((ROWS, CP)...  38.3 us
    unnamed x22, local copies, waits for them, and re-layouts  7.8 us

profile of v1, /device:TPU:1, one launch (start us, length us, event | category | flops | bytes accessed | tf_op | source)
XLA Modules:
  0.0 195.3 jit_solution(4612829684440347833)
XLA Ops:
  0.0 0.0 copy-start
  0.0 0.7 copy-done
  0.7 0.0 copy-start.2
  0.7 0.8 copy-done.2
  1.5 0.0 copy-start.5
  1.5 0.7 copy-done.5
  2.2 0.0 copy-start.6
  2.2 0.7 copy-done.6
  2.8 0.0 copy-start.10
  2.8 1.6 copy-done.10
  4.4 38.3 %teacher.1 = (bf16[8192,256]{1,0:T(8,128)(2,1)S(1)}, bf16[128,32,128]{2,1,0:T(8,128)(2,1)S(1)}, f32[8,256]{1,0:T(8,128)S(1)}) custom-call(s32[32,128]{1,0:T(8,128)S(1)} %bitcast.15, s32[128]{0:T(128)S(1)} %copy-done.5, bf16[8192,128]{1,0:T(8,128)(2,1)S(1)} %copy-done.10, bf16[172,128]{1,0:T(8,128)(2,1)S(1)} %bitcast.18, f32[1,172]{1,0:T(1,128)S(1)} %bitcast.23), custom_call_target="tpu_custom_call" | custom-call | flops 536870912 | bytes 8388608 | tf_op jit(solution)/shard_map/teacher/pallas_call | solution.py:165
  42.7 0.0 copy-start.3
  42.7 0.7 copy-done.3
  43.4 0.0 copy-start.4
  43.4 0.7 copy-done.4
  44.1 0.0 copy-start.7
  44.1 0.7 copy-done.7
  44.7 0.0 copy-start.8
  44.7 0.7 copy-done.8
  45.4 0.0 copy-start.9
  45.4 0.7 copy-done.9
  46.1 0.0 copy-start.1
  46.1 42.4 %first_step.1 = (bf16[64,128,256]{2,1,0:T(8,128)(2,1)S(1)}, bf16[64,128,256]{2,1,0:T(8,128)(2,1)S(1)}) custom-call(s32[64]{0:T(128)S(1)} %copy-done.4, s32[8,64]{1,0:T(8,128)S(1)} %bitcast.20, bf16[64,8,128,128]{3,2,1,0:T(8,128)(2,1)} %tiles_ref.5, bf16[64,128,256]{2,1,0:T(8,128)(2,1)S(1)} %bitcast.13, bf16[4096,128]{1,0:T(8,128)(2,1)S(1)} %bitcast.14, ...), custom_call_target="tpu_custom_call" | custom-call | flops 4294967296 | bytes 29360128 | tf_op jit(solution)/shard_map/first_step/pallas_call | solution.py:372
  88.5 0.0 copy-done.1
  88.5 28.9 %exchange.2.far_ref = bf16[128,48,128]{2,1,0:T(8,128)(2,1)S(1)} custom-call(s32[32,128]{1,0:T(8,128)S(1)} %bitcast.16, s32[128]{0:T(128)S(1)} %copy-done.5, bf16[8192,256]{1,0:T(8,128)(2,1)S(1)} %bitcast.12), custom_call_target="tpu_custom_call" | custom-call | bytes 8388608 | tf_op jit(solution)/shard_map/exchange/pallas_call | solution.py:232
  117.4 22.3 %later_step.1.labels_hbm = bf16[64,128,256]{2,1,0:T(8,128)(2,1)S(1)} custom-call(s32[64]{0:T(128)S(1)} %copy-done.4, s32[8,64]{1,0:T(8,128)S(1)} %bitcast.21, bf16[64,8,128,128]{3,2,1,0:T(8,128)(2,1)} %tiles_ref.5, bf16[64,128,256]{2,1,0:T(8,128)(2,1)S(1)} %get-tuple-element.13.labels_hbm, bf16[128,48,128]{2,1,0:T(8,128)(2,1)S(1)} %exchange.2.far_ref, ...), custom_call_target="tpu_custom_call" | custom-call | flops 4294967296 | bytes 29360128 | tf_op jit(solution)/shard_map/later_step/pallas_call | solution.py:402
  139.7 28.3 %exchange.3.far_ref = bf16[128,48,128]{2,1,0:T(8,128)(2,1)S(1)} custom-call(s32[32,128]{1,0:T(8,128)S(1)} %bitcast.17, s32[128]{0:T(128)S(1)} %copy-done.5, bf16[8192,256]{1,0:T(8,128)(2,1)S(1)} %bitcast.11), custom_call_target="tpu_custom_call" | custom-call | bytes 8388608 | tf_op jit(solution)/shard_map/exchange/pallas_call | solution.py:232
  167.9 27.4 %last_step.1 = f32[172,8192]{1,0:T(8,128)} custom-call(s32[64]{0:T(128)S(1)} %copy-done.4, s32[8,64]{1,0:T(8,128)S(1)} %bitcast.22, bf16[64,8,128,128]{3,2,1,0:T(8,128)(2,1)} %tiles_ref.5, bf16[64,128,256]{2,1,0:T(8,128)(2,1)S(1)} %later_step.1.labels_hbm, bf16[128,48,128]{2,1,0:T(8,128)(2,1)S(1)} %exchange.3.far_ref, ...), custom_call_target="tpu_custom_call" | custom-call | flops 4294967296 | bytes 29360128 | tf_op jit(solution)/shard_map/last_step/pallas_call | solution.py:402
Async XLA Ops:
  0.0 0.7 copy-start
  0.7 0.8 copy-start.2
  1.5 0.7 copy-start.5
  2.2 0.7 copy-start.6
  2.8 1.6 copy-start.10
  42.7 0.7 copy-start.3
  43.4 0.7 copy-start.4
  44.1 0.7 copy-start.7
  44.7 0.7 copy-start.8
  45.4 0.7 copy-start.9
  46.1 42.4 %copy-start.1 = (s32[128,32]{0,1:T(8,128)S(1)}, s32[128,32]{0,1:T(8,128)}, u32[]{:S(2)}) copy-start(s32[128,32]{0,1:T(8,128)} %param.15) | copy-start | bytes 49156

commit v2 on v0

v2 whole, which is shorter than its diff:
```python
import jax
import jax.numpy as jnp
from jax import lax
from jax.experimental import pallas as pl
from jax.experimental.pallas import tpu as pltpu
from jax.sharding import PartitionSpec as P

F = 128
C = 172
CP = 256
B = 128
RB = 64
TPR = 8
SLOT = 32
HALF = 128
PACK = 16
CHUNK = 1024
UNROLL = 8
HB = 32
ROWS = 8192
N = 128
NODES = ROWS * N

MOMENTUM = 0.7
PROPAGATE = 0.9
LOG_FLOOR = 0.0001
DEAD = 32768.0
LOW = -1e30
VMEM_LIMIT = 56 * 2**20
MESH = pl.DeviceIdType.MESH
MIX = 37
GROUP = 16
F32 = jnp.float32
BF16 = jnp.bfloat16


def in_hbm():
    return pl.BlockSpec(memory_space=pltpu.HBM)


def in_vmem():
    return pl.BlockSpec(memory_space=pltpu.VMEM)


def propagate_kernel(
    rows_hbm, cnt_hbm, feat_hbm, wt_hbm, b_hbm, ema_hbm, target_hbm, tiles_hbm, col_hbm, used_hbm,
    wide_a, wide_b,
    rows_v, rows_w, rows, cnt, feat, wt, bias, ema, target, tiles, col, used,
    wpad, bpad, epad, tpad, stage,
    seed_a, seed_b, one_a, one_b, two_a, two_b,
    feat_send, feat_recv, send_a1, send_a2, send_b1, send_b2, recv_b1, recv_b2,
    part1, part2, load_sem, flip_sem, send_sem, recv_sem,
):
    me = lax.axis_index("dom")
    next_door = lax.rem(me + 1, N)

    loads = [
        pltpu.make_async_copy(src, dst, load_sem.at[i])
        for i, (src, dst) in enumerate(
            (
                (rows_hbm, rows_v), (feat_hbm, feat), (cnt_hbm, cnt), (wt_hbm, wt), (b_hbm, bias), (ema_hbm, ema),
                (target_hbm, target), (col_hbm, col), (used_hbm, used), (tiles_hbm, tiles),
            )
        )
    ]
    for load in loads:
        load.start()

    barrier = pltpu.get_barrier_semaphore()

    def tell(k, carry):
        pl.semaphore_signal(barrier, inc=1, device_id=(lax.rem(me + k, N),), device_id_type=MESH)
        return carry

    lax.fori_loop(1, N, tell, 0)

    loads[0].wait()
    rows_w[...] = jnp.concatenate([rows_v[...], jnp.zeros((B - SLOT, N), jnp.int32)], axis=0).T
    flip = pltpu.make_async_copy(rows_w, rows, flip_sem)
    flip.start()
    loads[1].wait()

    def widen(k, carry):
        at = pl.multiple_of(k * CHUNK, CHUNK)
        wide_a[pl.ds(at, CHUNK), :] = feat[pl.ds(at, CHUNK), :].astype(F32)
        return carry

    lax.fori_loop(0, ROWS // CHUNK, widen, 0)
    for load in loads[2:9]:
        load.wait()
    flip.wait()

    def picked(wide, dest, dead):
        for j in range(SLOT):
            stage[pl.ds(j, 1), :] = wide[pl.ds(rows[dest, j], 1), :]
        live = lax.broadcasted_iota(jnp.int32, (SLOT, HALF), 0) < cnt[dest]
        return jnp.where(live, stage[...], dead)

    def packed(values):
        lane = lax.broadcasted_iota(jnp.int32, (PACK, HALF), 1)
        return jnp.where(lane < HALF // 2, values[:PACK], pltpu.roll(values[PACK:], HALF // 2, 1))

    def spread(make, sendbuf, landing, number):
        def send(k, carry):
            dest = lax.rem(me + lax.rem(k * MIX, N), N)
            sendbuf[pl.ds(k, 1)] = make(dest)[None]
            pltpu.make_async_remote_copy(
                src_ref=sendbuf.at[k], dst_ref=landing, send_sem=send_sem.at[number], recv_sem=recv_sem.at[number],
                device_id=(dest,), device_id_type=MESH,
            ).start()
            return carry

        lax.fori_loop(1, N, send, 0)
        whole = sendbuf.at[pl.ds(0, N - 1)]
        return pltpu.make_async_remote_copy(
            src_ref=whole, dst_ref=whole, send_sem=send_sem.at[number], recv_sem=recv_sem.at[number],
            device_id=(next_door,), device_id_type=MESH,
        )

    block_me = RB + me // (B // SLOT)
    row_me = pl.multiple_of(lax.rem(me, B // SLOT) * SLOT, SLOT)

    def own_place(labels):
        return labels.at[block_me, pl.ds(row_me, SLOT), :]

    def put_own(labels, values):
        labels[pl.ds(block_me, 1), pl.ds(row_me, SLOT), :] = values[None]

    def feature_rows(dest):
        return picked(wide_a, dest, DEAD).astype(BF16)

    def rows_a(dest):
        return picked(wide_a, dest, 0.0).astype(BF16)

    def rows_b(dest):
        return packed(picked(wide_b, dest, 0.0)).astype(BF16)

    feat_recv[pl.ds(me, 1)] = feature_rows(me)[None]
    pl.semaphore_wait(barrier, N - 1)
    features_sent = spread(feature_rows, feat_send, feat_recv.at[me], 0)

    wpad[...] = jnp.zeros_like(wpad)
    wpad[pl.ds(0, C), :] = wt[...].astype(F32)
    bpad[...] = jnp.full(bpad.shape, LOW, F32)
    bpad[:, pl.ds(0, C)] = bias[...]
    epad[...] = jnp.full(epad.shape, 1.0, F32)
    epad[:, pl.ds(0, C)] = ema[...]
    tpad[...] = jnp.zeros_like(tpad)
    tpad[:, pl.ds(0, C)] = target[...]
    weights = wpad[...].astype(BF16)
    blocks = CHUNK // B

    def soft(values):
        logits = lax.dot_general(values, weights, (((1,), (1,)), ((), ())), preferred_element_type=F32) + bpad[...]
        e = jnp.exp(logits - jnp.max(logits, axis=-1, keepdims=True))
        return e * (1.0 / jnp.sum(e, axis=-1, keepdims=True))

    def keep(first, values):
        seed_a[pl.ds(first, blocks)] = values[:, :HALF].reshape(blocks, B, HALF)
        seed_b[pl.ds(first, blocks)] = values[:, HALF:].reshape(blocks, B, HALF)

    def local(k, acc):
        p = soft(feat[pl.ds(pl.multiple_of(k * CHUNK, CHUNK), CHUNK), :]).astype(BF16)
        keep(k * blocks, p)
        return acc + jnp.sum(p.astype(F32).reshape(CHUNK // 8, 8, CP), axis=0)

    acc = lax.fori_loop(0, ROWS // CHUNK, local, jnp.zeros((8, CP), F32))

    group = me // GROUP
    place = lax.rem(me, GROUP)
    groups = N // GROUP
    part1[pl.ds(place, 1)] = acc[None]

    def send_near(k, carry):
        pltpu.make_async_remote_copy(
            src_ref=part1.at[place], dst_ref=part1.at[place], send_sem=send_sem.at[5], recv_sem=recv_sem.at[5],
            device_id=(group * GROUP + lax.rem(place + k, GROUP),), device_id_type=MESH,
        ).start()
        return carry

    lax.fori_loop(1, GROUP, send_near, 0)
    near = pltpu.make_async_remote_copy(
        src_ref=part1.at[pl.ds(0, GROUP - 1)], dst_ref=part1.at[pl.ds(0, GROUP - 1)],
        send_sem=send_sem.at[5], recv_sem=recv_sem.at[5], device_id=(next_door,), device_id_type=MESH,
    )
    near.wait_recv()
    part2[pl.ds(group, 1)] = jnp.sum(part1[...], axis=0)[None]

    def send_far(k, carry):
        pltpu.make_async_remote_copy(
            src_ref=part2.at[group], dst_ref=part2.at[group], send_sem=send_sem.at[6], recv_sem=recv_sem.at[6],
            device_id=(lax.rem(group + k, groups) * GROUP + place,), device_id_type=MESH,
        ).start()
        return carry

    lax.fori_loop(1, groups, send_far, 0)
    far = pltpu.make_async_remote_copy(
        src_ref=part2.at[pl.ds(0, groups - 1)], dst_ref=part2.at[pl.ds(0, groups - 1)],
        send_sem=send_sem.at[6], recv_sem=recv_sem.at[6], device_id=(next_door,), device_id_type=MESH,
    )

    features_sent.wait_recv()
    sources = CHUNK // SLOT

    def boundary(k, carry):
        f = feat_recv[pl.ds(k * sources, sources)].reshape(CHUNK, F)
        live = f[:, :1].astype(F32) < DEAD / 2
        keep(RB + k * blocks, jnp.where(live, soft(f), 0.0).astype(BF16))
        return carry

    lax.fori_loop(0, HB * B // CHUNK, boundary, 0)
    far.wait_recv()
    total = jnp.sum(jnp.sum(part2[...], axis=0), axis=0, keepdims=True)
    ratio = tpad[...] / (MOMENTUM * epad[...] + (1.0 - MOMENTUM) * total / NODES)

    def align(k, carry):
        a = seed_a[pl.ds(k * blocks, blocks)].reshape(CHUNK, HALF).astype(F32) * ratio[:, :HALF]
        b = seed_b[pl.ds(k * blocks, blocks)].reshape(CHUNK, HALF).astype(F32) * ratio[:, HALF:]
        row_total = jnp.sum(a + b, axis=-1, keepdims=True)
        scale = 1.0 / jnp.where(row_total > 0.0, row_total, 1.0)
        seed_a[pl.ds(k * blocks, blocks)] = (a * scale).astype(BF16).reshape(blocks, B, HALF)
        seed_b[pl.ds(k * blocks, blocks)] = (b * scale).astype(BF16).reshape(blocks, B, HALF)
        return carry

    lax.fori_loop(0, (RB + HB) * B // CHUNK, align, 0)
    for labels in (seed_a, seed_b, one_a, one_b, two_a, two_b):
        labels[pl.ds(RB + HB, 1)] = jnp.zeros((1, B, HALF), BF16)
    loads[9].wait()

    def multiply(labels, seed, following, wide):
        def several(i, carry):
            for u in range(UNROLL):
                r = i * UNROLL + u
                count = used[r]
                lhs = jnp.concatenate([tiles[r, t] for t in range(TPR)], axis=1)
                rhs = jnp.concatenate(
                    [labels[jnp.where(t < count, col[t, r], RB + HB)] for t in range(TPR)], axis=0
                )
                mixed = jnp.dot(lhs, rhs, preferred_element_type=F32)
                current = PROPAGATE * mixed + (1.0 - PROPAGATE) * seed[r].astype(F32)
                wide[pl.ds(pl.multiple_of(r * B, B), B), :] = current
                if following is not None:
                    following[pl.ds(r, 1)] = current.astype(BF16)[None]
            return carry

        lax.fori_loop(0, RB // UNROLL, several, 0)

    def unpack(received, labels):
        def several(h, carry):
            x = received[pl.ds(h * (B // SLOT), B // SLOT)].astype(F32)
            left = lax.broadcasted_iota(jnp.int32, x.shape, 2) < HALF // 2
            first = jnp.where(left, x, 0.0)
            second = jnp.where(left, pltpu.roll(x, HALF // 2, 2), 0.0)
            both = jnp.concatenate([first, second], axis=1).astype(BF16)
            labels[pl.ds(RB + h, 1)] = both.reshape(1, B, HALF)
            return carry

        lax.fori_loop(0, HB, several, 0, unroll=4)

    multiply(seed_a, seed_a, one_a, wide_a)
    put_own(one_a, rows_a(me))
    sent_a1 = spread(rows_a, send_a1, own_place(one_a), 1)
    multiply(seed_b, seed_b, one_b, wide_b)
    recv_b1[pl.ds(me, 1)] = rows_b(me)[None]
    sent_b1 = spread(rows_b, send_b1, recv_b1.at[me], 2)

    sent_a1.wait_recv()
    multiply(one_a, seed_a, two_a, wide_a)
    put_own(two_a, rows_a(me))
    sent_a2 = spread(rows_a, send_a2, own_place(two_a), 3)
    sent_b1.wait_recv()
    unpack(recv_b1, one_b)
    multiply(one_b, seed_b, two_b, wide_b)
    recv_b2[pl.ds(me, 1)] = rows_b(me)[None]
    sent_b2 = spread(rows_b, send_b2, recv_b2.at[me], 4)

    sent_a2.wait_recv()
    multiply(two_a, seed_a, None, wide_a)
    sent_b2.wait_recv()
    unpack(recv_b2, two_b)
    multiply(two_b, seed_b, None, wide_b)
    for sent in (near, far, features_sent, sent_a1, sent_b1, sent_a2, sent_b2):
        sent.wait_send()


def propagate(rows_t, counts, features, wt, bias, ema, target, tiles, cols_t, used):
    wide = jax.ShapeDtypeStruct((ROWS, HALF), F32)
    labels = pltpu.VMEM((RB + HB + 1, B, HALF), BF16)
    slots = pltpu.VMEM((N, SLOT, HALF), BF16)
    small = pltpu.VMEM((N, PACK, HALF), BF16)
    row = pltpu.VMEM((1, CP), F32)
    vector = pltpu.VMEM((1, C), F32)
    return pl.pallas_call(
        propagate_kernel,
        out_shape=(wide, wide),
        in_specs=[in_hbm()] * 10,
        out_specs=(in_vmem(), in_vmem()),
        scratch_shapes=[
            pltpu.VMEM((SLOT, N), jnp.int32),
            pltpu.VMEM((N, B), jnp.int32),
            pltpu.SMEM((N, B), jnp.int32),
            pltpu.SMEM((N,), jnp.int32),
            pltpu.VMEM((ROWS, F), BF16),
            pltpu.VMEM((C, F), BF16),
            vector, vector, vector,
            pltpu.VMEM((RB, TPR, B, B), BF16),
            pltpu.SMEM((TPR, RB), jnp.int32),
            pltpu.SMEM((RB,), jnp.int32),
            pltpu.VMEM((CP, F), F32),
            row, row, row,
            pltpu.VMEM((SLOT, HALF), F32),
            labels, labels, labels, labels, labels, labels,
            slots, slots, slots, slots, small, small, small, small,
            pltpu.VMEM((GROUP, 8, CP), F32),
            pltpu.VMEM((N // GROUP, 8, CP), F32),
            pltpu.SemaphoreType.DMA((10,)),
            pltpu.SemaphoreType.DMA,
            pltpu.SemaphoreType.DMA((7,)),
            pltpu.SemaphoreType.DMA((7,)),
        ],
        compiler_params=pltpu.CompilerParams(collective_id=0, has_side_effects=True, vmem_limit_bytes=VMEM_LIMIT),
        cost_estimate=pl.CostEstimate(
            flops=6 * RB * TPR * B * B * CP, bytes_accessed=24 * 2**20, transcendentals=(ROWS + HB * B) * CP
        ),
        name="propagate",
    )(rows_t, counts, features, wt, bias, ema, target, tiles, cols_t, used)


LOG_ROWS = 1024


def log_kernel(a_ref, b_ref, out_ref):
    for i in range(LOG_ROWS // B):
        a = a_ref[pl.ds(i * B, B), :].T
        b = b_ref[pl.ds(i * B, B), :].T
        out_ref[pl.ds(0, HALF), pl.ds(i * B, B)] = jnp.log(a + LOG_FLOOR)
        out_ref[pl.ds(HALF, C - HALF), pl.ds(i * B, B)] = jnp.log(b[: C - HALF] + LOG_FLOOR)


def log_scores(a, b):
    part = pl.BlockSpec((LOG_ROWS, HALF), lambda i: (i, 0))
    return pl.pallas_call(
        log_kernel,
        grid=(ROWS // LOG_ROWS,),
        out_shape=jax.ShapeDtypeStruct((C, ROWS), F32),
        in_specs=[part, part],
        out_specs=pl.BlockSpec((C, LOG_ROWS), lambda i: (0, i)),
        compiler_params=pltpu.CompilerParams(vmem_limit_bytes=VMEM_LIMIT),
        cost_estimate=pl.CostEstimate(flops=0, bytes_accessed=14 * 2**20, transcendentals=ROWS * C),
        name="log_scores",
    )(a, b)


def on_device(
    features, teacher_w, teacher_b, ema_prior, target_prior, send_rows, send_count, tiles, tile_col, tile_count
):
    a, b = propagate(
        send_rows.T, send_count, features, teacher_w.T, teacher_b.reshape(1, C), ema_prior.reshape(1, C),
        target_prior.reshape(1, C), tiles, tile_col.T, tile_count,
    )
    return log_scores(a, b).T


def solution(mesh):
    placed = (
        P("dom", None), P(), P(), P(), P(), P("dom", None), P("dom"),
        P("dom", None, None, None), P("dom", None), P("dom"),
    )
    return jax.shard_map(on_device, mesh=mesh, in_specs=placed, out_specs=P("dom", None), check_vma=False)
```

time: 425 us -> 117 us (0.28); the launches traced: 418 us -> 117 us
  local copies, waits for them, and re-layouts: 158 us -> 0 us
  Pallas kernels: 0 us -> 117 us
  blocking collectives: 68.6 us -> 0 us
  other arithmetic: 66.5 us -> 0 us
  waiting for transfers between devices: 62.9 us -> 0 us
  matrix products: 46.9 us -> 0 us
  starting transfers between devices: 14.2 us -> 0 us
    pallas_call x0 -> x2, Pallas kernels: none -> 117 us  [the longest x1 108 us: propagate(): pl.pallas_call(propagate_kernel, out_shape=(wide, wide), in_specs=[in_hbm...]
    gather x6 -> x0, local copies, waits for them, and re-layouts: 101 us -> none  [the longest x3 53.9 us: on_device(): picked_blocks = blocks[tile_col]]
    psum x1 -> x0, blocking collectives: 68.6 us -> none  [on_device(): marginal_sum = lax.psum(local_marginal, 'dom')]
    all_to_all x3 -> x0, waiting for transfers between devices: 62.9 us -> none  [send_boundary(): lax.all_to_all(picked, 'dom', split_axis=0, concat_axis=0, tiled=True)]
    dot_general x4 -> x0, matrix products: 46.9 us -> none  [the longest x3 45.1 us: on_device(): jnp.einsum('rtij,rtcj->rci', live_tiles, picked_blocks, preferred_element...]
    convert_element_type x4 -> x0, other arithmetic: 30.2 us -> none  [on_device(): label_columns = current_columns.astype(jnp.bfloat16)]
    unnamed x32 -> x0, local copies, waits for them, and re-layouts: 20.4 us -> none
    all_to_all x3 -> x0, starting transfers between devices: 14.2 us -> none  [send_boundary(): lax.all_to_all(picked, 'dom', split_axis=0, concat_axis=0, tiled=True)]
  transfers between devices with their start and end apart: 3 -> 0, of which waited for: 3 -> 0; matrix products, arithmetic and copies ran while one was open for 7% -> 0% of each run, Pallas kernels for 0% -> 0%
where the time goes in v2:
time: 117 us
  Pallas kernels  117 us (100%)
    pallas_call x1, Pallas kernels, propagate(): pl.pallas_call(propagate_kernel, out_shape=(wide, wide), in_specs=[in_hbm...  108 us
    pallas_call x1, Pallas kernels, log_scores(): pl.pallas_call(log_kernel, grid=(ROWS // LOG_ROWS,), out_shape=jax.ShapeD...  9.04 us

profile of v2, /device:TPU:1, one launch (start us, length us, event | category | flops | bytes accessed | tf_op | source)
XLA Modules:
  0.0 117.0 jit_solution(121333743259921481)
XLA Ops:
  0.0 107.9 %propagate.1 = (f32[8192,128]{1,0:T(8,128)}, f32[8192,128]{1,0:T(8,128)}) custom-call(s32[32,128]{1,0:T(8,128)} %bitcast.8, s32[128]{0:T(128)} %cnt_hbm.1, bf16[8192,128]{1,0:T(8,128)(2,1)} %feat_hbm.1, bf16[172,128]{1,0:T(8,128)(2,1)} %bitcast.7, f32[1,172]{1,0:T(1,128)} %bitcast.10, f32[1,172]{1,0:T(1,128)} %bitcast.11, f32[1,172]{1,0:T(1,128)} %bitcast.12, ...), custom_call_target="tpu_custom_call" | custom-call | flops 12884901888 | bytes 25165824 | tf_op jit(solution)/shard_map/propagate/pallas_call | solution.py:293
  107.9 9.0 %log_scores.1 = f32[172,8192]{1,0:T(8,128)} custom-call(f32[8192,128]{1,0:T(8,128)} %get-tuple-element.7.a_ref, f32[8192,128]{1,0:T(8,128)} %get-tuple-element.8.b_ref), custom_call_target="tpu_custom_call" | custom-call | bytes 14680064 | tf_op jit(solution)/shard_map/log_scores/pallas_call | solution.py:342

commit v3 on v2

v3 whole, which is shorter than its diff:
```python
import jax
import jax.numpy as jnp
from jax import lax
from jax.experimental import pallas as pl
from jax.experimental.pallas import tpu as pltpu
from jax.sharding import PartitionSpec as P

F = 128
C = 172
CP = 256
B = 128
RB = 64
TPR = 8
SLOT = 32
HALF = 128
PACK = 16
CHUNK = 1024
UNROLL = 8
HB = 32
ROWS = 8192
N = 128
NODES = ROWS * N

MOMENTUM = 0.7
PROPAGATE = 0.9
LOG_FLOOR = 0.0001
DEAD = 32768.0
LOW = -1e30
VMEM_LIMIT = 58 * 2**20
GANG = 8
MESH = pl.DeviceIdType.MESH
MIX = 37
GROUP = 16
F32 = jnp.float32
BF16 = jnp.bfloat16


def in_hbm():
    return pl.BlockSpec(memory_space=pltpu.HBM)


def in_vmem():
    return pl.BlockSpec(memory_space=pltpu.VMEM)


def propagate_kernel(
    rows_hbm, cnt_hbm, feat_hbm, wt_hbm, b_hbm, ema_hbm, target_hbm, tiles_hbm, col_hbm, used_hbm,
    out_ref,
    wide_a, wide_b, rows_v, rows_w, rows, cnt, feat, wt, bias, ema, target, tiles, col, used,
    wpad, bpad, epad, tpad,
    seed_a, seed_b, one_a, one_b, two_a, two_b,
    send_a, send_b, feat_recv, recv_b1, recv_b2,
    part1, part2, load_sem, flip_sem, send_sem, recv_sem,
):
    me = lax.axis_index("dom")
    next_door = lax.rem(me + 1, N)

    loads = [
        pltpu.make_async_copy(src, dst, load_sem.at[i])
        for i, (src, dst) in enumerate(
            (
                (rows_hbm, rows_v), (feat_hbm, feat), (cnt_hbm, cnt), (wt_hbm, wt), (b_hbm, bias), (ema_hbm, ema),
                (target_hbm, target), (col_hbm, col), (used_hbm, used), (tiles_hbm, tiles),
            )
        )
    ]
    for load in loads[:9]:
        load.start()

    barrier = pltpu.get_barrier_semaphore()

    def tell(k, carry):
        pl.semaphore_signal(barrier, inc=1, device_id=(lax.rem(me + k, N),), device_id_type=MESH)
        return carry

    lax.fori_loop(1, N, tell, 0)

    loads[0].wait()
    rows_w[...] = jnp.concatenate([rows_v[...], jnp.zeros((B - SLOT, N), jnp.int32)], axis=0).T
    flip = pltpu.make_async_copy(rows_w, rows, flip_sem)
    flip.start()
    loads[1].wait()

    def widen(k, carry):
        at = pl.multiple_of(k * CHUNK, CHUNK)
        wide_a[pl.ds(at, CHUNK), :] = feat[pl.ds(at, CHUNK), :].astype(F32)
        return carry

    lax.fori_loop(0, ROWS // CHUNK, widen, 0)
    for load in loads[2:9]:
        load.wait()
    flip.wait()

    def picked(wide, dest, dead):
        taken = jnp.concatenate([wide[pl.ds(rows[dest, j], 1), :] for j in range(SLOT)], axis=0)
        live = lax.broadcasted_iota(jnp.int32, (SLOT, HALF), 0) < cnt[dest]
        return jnp.where(live, taken, dead)

    def packed(values):
        lane = lax.broadcasted_iota(jnp.int32, (PACK, HALF), 1)
        return jnp.where(lane < HALF // 2, values[:PACK], pltpu.roll(values[PACK:], HALF // 2, 1))

    def spread(make, sendbuf, landing, number, first=0, last=N):
        def gang(base, turns):
            dests = [lax.rem(me + lax.rem((base + u) * MIX, N), N) for u in turns]
            for u, dest in zip(turns, dests):
                sendbuf[pl.ds(base + u, 1)] = make(dest)[None]
            for u, dest in zip(turns, dests):
                pltpu.make_async_remote_copy(
                    src_ref=sendbuf.at[base + u], dst_ref=landing(base + u),
                    send_sem=send_sem.at[number], recv_sem=recv_sem.at[number],
                    device_id=(dest,), device_id_type=MESH,
                ).start()

        def several(i, carry):
            gang(i * GANG, range(GANG))
            return carry

        if first == 0:
            gang(0, range(1, GANG))
        lax.fori_loop(max(first // GANG, 1), last // GANG, several, 0)
        whole = sendbuf.at[pl.ds(0, last - max(first, 1))]
        return pltpu.make_async_remote_copy(
            src_ref=whole, dst_ref=whole, send_sem=send_sem.at[number], recv_sem=recv_sem.at[number],
            device_id=(next_door,), device_id_type=MESH,
        )

    block_me = RB + me // (B // SLOT)
    row_me = pl.multiple_of(lax.rem(me, B // SLOT) * SLOT, SLOT)

    def own_place(labels):
        return lambda turn: labels.at[block_me, pl.ds(row_me, SLOT), :]

    def put_own(labels, values):
        labels[pl.ds(block_me, 1), pl.ds(row_me, SLOT), :] = values[None]

    def feature_rows(dest):
        return picked(wide_a, dest, DEAD).astype(BF16)

    def rows_a(dest):
        return picked(wide_a, dest, 0.0).astype(BF16)

    def rows_b(dest):
        return packed(picked(wide_b, dest, 0.0)).astype(BF16)

    wpad[...] = jnp.zeros_like(wpad)
    wpad[pl.ds(0, C), :] = wt[...].astype(F32)
    bpad[...] = jnp.full(bpad.shape, LOW, F32)
    bpad[:, pl.ds(0, C)] = bias[...]
    epad[...] = jnp.full(epad.shape, 1.0, F32)
    epad[:, pl.ds(0, C)] = ema[...]
    tpad[...] = jnp.zeros_like(tpad)
    tpad[:, pl.ds(0, C)] = target[...]
    weights = wpad[...].astype(BF16)
    blocks = CHUNK // B

    def soft(values):
        logits = lax.dot_general(values, weights, (((1,), (1,)), ((), ())), preferred_element_type=F32) + bpad[...]
        e = jnp.exp(logits - jnp.max(logits, axis=-1, keepdims=True))
        return e * (1.0 / jnp.sum(e, axis=-1, keepdims=True))

    def local(k, acc):
        p = soft(feat[pl.ds(pl.multiple_of(k * CHUNK, CHUNK), CHUNK), :]).astype(BF16)
        seed_a[pl.ds(k * blocks, blocks)] = p[:, :HALF].reshape(blocks, B, HALF)
        seed_b[pl.ds(k * blocks, blocks)] = p[:, HALF:].reshape(blocks, B, HALF)
        return acc + jnp.sum(p.astype(F32).reshape(CHUNK // 8, 8, CP), axis=0)

    acc = lax.fori_loop(0, ROWS // CHUNK, local, jnp.zeros((8, CP), F32))
    pl.semaphore_wait(barrier, N - 1)

    group = me // GROUP
    place = lax.rem(me, GROUP)
    groups = N // GROUP
    part1[pl.ds(place, 1)] = acc[None]

    def send_near(k, carry):
        pltpu.make_async_remote_copy(
            src_ref=part1.at[place], dst_ref=part1.at[place], send_sem=send_sem.at[5], recv_sem=recv_sem.at[5],
            device_id=(group * GROUP + lax.rem(place + k, GROUP),), device_id_type=MESH,
        ).start()
        return carry

    lax.fori_loop(1, GROUP, send_near, 0)
    near = pltpu.make_async_remote_copy(
        src_ref=part1.at[pl.ds(0, GROUP - 1)], dst_ref=part1.at[pl.ds(0, GROUP - 1)],
        send_sem=send_sem.at[5], recv_sem=recv_sem.at[5], device_id=(next_door,), device_id_type=MESH,
    )

    def landing(turn):
        return feat_recv.at[turn]

    feat_recv[pl.ds(0, 1)] = feature_rows(me)[None]
    early = spread(feature_rows, send_a, landing, 0, 0, N // 2)
    near.wait_recv()
    part2[pl.ds(group, 1)] = jnp.sum(part1[...], axis=0)[None]

    def send_far(k, carry):
        pltpu.make_async_remote_copy(
            src_ref=part2.at[group], dst_ref=part2.at[group], send_sem=send_sem.at[6], recv_sem=recv_sem.at[6],
            device_id=(lax.rem(group + k, groups) * GROUP + place,), device_id_type=MESH,
        ).start()
        return carry

    lax.fori_loop(1, groups, send_far, 0)
    far = pltpu.make_async_remote_copy(
        src_ref=part2.at[pl.ds(0, groups - 1)], dst_ref=part2.at[pl.ds(0, groups - 1)],
        send_sem=send_sem.at[6], recv_sem=recv_sem.at[6], device_id=(next_door,), device_id_type=MESH,
    )
    late = spread(feature_rows, send_a, landing, 7, N // 2, N)
    loads[9].start()
    for labels in (seed_a, seed_b, one_a, one_b, two_a, two_b):
        labels[pl.ds(RB + HB, 1)] = jnp.zeros((1, B, HALF), BF16)

    far.wait_recv()
    total = jnp.sum(jnp.sum(part2[...], axis=0), axis=0, keepdims=True)
    ratio = tpad[...] / (MOMENTUM * epad[...] + (1.0 - MOMENTUM) * total / NODES)

    def aligned(p_a, p_b):
        a = p_a.astype(F32) * ratio[:, :HALF]
        b = p_b.astype(F32) * ratio[:, HALF:]
        row_total = jnp.sum(a + b, axis=-1, keepdims=True)
        scale = 1.0 / jnp.where(row_total > 0.0, row_total, 1.0)
        return (a * scale).astype(BF16), (b * scale).astype(BF16)

    def align(k, carry):
        a, b = aligned(
            seed_a[pl.ds(k * blocks, blocks)].reshape(CHUNK, HALF), seed_b[pl.ds(k * blocks, blocks)].reshape(CHUNK, HALF)
        )
        seed_a[pl.ds(k * blocks, blocks)] = a.reshape(blocks, B, HALF)
        seed_b[pl.ds(k * blocks, blocks)] = b.reshape(blocks, B, HALF)
        return carry

    lax.fori_loop(0, RB * B // CHUNK, align, 0)

    sources = CHUNK // SLOT

    def boundary(k, carry):
        f = feat_recv[pl.ds(k * sources, sources)].reshape(CHUNK, F)
        live = f[:, :1].astype(F32) < DEAD / 2
        p = jnp.where(live, soft(f), 0.0).astype(BF16)
        a, b = aligned(p[:, :HALF], p[:, HALF:])
        for u in range(sources):
            source = lax.rem(me + N - lax.rem((k * sources + u) * MIX, N), N)
            block = RB + source // (B // SLOT)
            row = pl.multiple_of(lax.rem(source, B // SLOT) * SLOT, SLOT)
            seed_a[pl.ds(block, 1), pl.ds(row, SLOT), :] = a[u * SLOT : (u + 1) * SLOT][None]
            seed_b[pl.ds(block, 1), pl.ds(row, SLOT), :] = b[u * SLOT : (u + 1) * SLOT][None]
        return carry

    turns = N // sources
    early.wait_recv()
    lax.fori_loop(0, turns // 2, boundary, 0)
    late.wait_recv()
    lax.fori_loop(turns // 2, turns, boundary, 0)
    loads[9].wait()

    def multiply(labels, seeds, following, wides):
        def several(i, carry):
            for u in range(UNROLL):
                r = i * UNROLL + u
                count = used[r]
                lhs = jnp.concatenate([tiles[r, t] for t in range(TPR)], axis=1)
                cols = [jnp.where(t < count, col[t, r], RB + HB) for t in range(TPR)]
                rhs = jnp.concatenate([jnp.concatenate([part[c] for part in labels], axis=1) for c in cols], axis=0)
                mixed = jnp.dot(lhs, rhs, preferred_element_type=F32)
                for q, seed in enumerate(seeds):
                    own = mixed[:, q * HALF : (q + 1) * HALF]
                    current = PROPAGATE * own + (1.0 - PROPAGATE) * seed[r].astype(F32)
                    at = pl.multiple_of(r * B, B)
                    if following:
                        wides[q][pl.ds(at, B), :] = current
                        following[q][pl.ds(r, 1)] = current.astype(BF16)[None]
                    else:
                        low, high = q * HALF, min((q + 1) * HALF, C)
                        out_ref[pl.ds(low, high - low), pl.ds(at, B)] = jnp.log(current.T[: high - low] + LOG_FLOOR)
            return carry

        lax.fori_loop(0, RB // UNROLL, several, 0)

    def unpack(received, labels):
        def several(h, carry):
            x = received[pl.ds(h * (B // SLOT), B // SLOT)].astype(F32)
            left = lax.broadcasted_iota(jnp.int32, x.shape, 2) < HALF // 2
            first = jnp.where(left, x, 0.0)
            second = jnp.where(left, pltpu.roll(x, HALF // 2, 2), 0.0)
            both = jnp.concatenate([first, second], axis=1).astype(BF16)
            labels[pl.ds(RB + h, 1)] = both.reshape(1, B, HALF)
            return carry

        lax.fori_loop(0, HB, several, 0, unroll=4)

    def here(received):
        return lambda turn: received.at[me]

    multiply((seed_a, seed_b), (seed_a, seed_b), (one_a, one_b), (wide_a, wide_b))
    early.wait_send()
    late.wait_send()
    put_own(one_a, rows_a(me))
    sent_a1 = spread(rows_a, send_a, own_place(one_a), 1)
    recv_b1[pl.ds(me, 1)] = rows_b(me)[None]
    sent_b1 = spread(rows_b, send_b, here(recv_b1), 2)

    sent_a1.wait_recv()
    multiply((one_a,), (seed_a,), (two_a,), (wide_a,))
    sent_a1.wait_send()
    put_own(two_a, rows_a(me))
    sent_a2 = spread(rows_a, send_a, own_place(two_a), 3)
    sent_b1.wait_recv()
    unpack(recv_b1, one_b)
    multiply((one_b,), (seed_b,), (two_b,), (wide_b,))
    sent_b1.wait_send()
    recv_b2[pl.ds(me, 1)] = rows_b(me)[None]
    sent_b2 = spread(rows_b, send_b, here(recv_b2), 4)

    sent_a2.wait_recv()
    sent_b2.wait_recv()
    unpack(recv_b2, two_b)
    multiply((two_a, two_b), (seed_a, seed_b), (), ())
    for sent in (near, far, sent_a2, sent_b2):
        sent.wait_send()


def propagate(rows_t, counts, features, wt, bias, ema, target, tiles, cols_t, used):
    wide = pltpu.VMEM((ROWS, HALF), F32)
    labels = pltpu.VMEM((RB + HB + 1, B, HALF), BF16)
    slots = pltpu.VMEM((N, SLOT, HALF), BF16)
    small = pltpu.VMEM((N, PACK, HALF), BF16)
    row = pltpu.VMEM((1, CP), F32)
    vector = pltpu.VMEM((1, C), F32)
    return pl.pallas_call(
        propagate_kernel,
        out_shape=jax.ShapeDtypeStruct((C, ROWS), F32),
        in_specs=[in_hbm()] * 10,
        out_specs=in_vmem(),
        scratch_shapes=[
            wide, wide,
            pltpu.VMEM((SLOT, N), jnp.int32),
            pltpu.VMEM((N, B), jnp.int32),
            pltpu.SMEM((N, B), jnp.int32),
            pltpu.SMEM((N,), jnp.int32),
            pltpu.VMEM((ROWS, F), BF16),
            pltpu.VMEM((C, F), BF16),
            vector, vector, vector,
            pltpu.VMEM((RB, TPR, B, B), BF16),
            pltpu.SMEM((TPR, RB), jnp.int32),
            pltpu.SMEM((RB,), jnp.int32),
            pltpu.VMEM((CP, F), F32),
            row, row, row,
            labels, labels, labels, labels, labels, labels,
            slots, small, slots, small, small,
            pltpu.VMEM((GROUP, 8, CP), F32),
            pltpu.VMEM((N // GROUP, 8, CP), F32),
            pltpu.SemaphoreType.DMA((10,)),
            pltpu.SemaphoreType.DMA,
            pltpu.SemaphoreType.DMA((8,)),
            pltpu.SemaphoreType.DMA((8,)),
        ],
        compiler_params=pltpu.CompilerParams(collective_id=0, has_side_effects=True, vmem_limit_bytes=VMEM_LIMIT),
        cost_estimate=pl.CostEstimate(
            flops=6 * RB * TPR * B * B * CP, bytes_accessed=24 * 2**20, transcendentals=(ROWS + HB * B) * CP
        ),
        name="propagate",
    )(rows_t, counts, features, wt, bias, ema, target, tiles, cols_t, used)


def on_device(
    features, teacher_w, teacher_b, ema_prior, target_prior, send_rows, send_count, tiles, tile_col, tile_count
):
    out_t = propagate(
        send_rows.T, send_count, features, teacher_w.T, teacher_b.reshape(1, C), ema_prior.reshape(1, C),
        target_prior.reshape(1, C), tiles, tile_col.T, tile_count,
    )
    return out_t.T


def solution(mesh):
    placed = (
        P("dom", None), P(), P(), P(), P(), P("dom", None), P("dom"),
        P("dom", None, None, None), P("dom", None), P("dom"),
    )
    return jax.shard_map(on_device, mesh=mesh, in_specs=placed, out_specs=P("dom", None), check_vma=False)
```

time: 117 us -> 104 us (0.89)
  Pallas kernels: 117 us -> 98.2 us
  local copies, waits for them, and re-layouts: 0 us -> 5.77 us
    pallas_call x2 -> x1, Pallas kernels: 117 us -> 98.2 us  [propagate(): pl.pallas_call(propagate_kernel, out_shape=jax.ShapeDtypeStruct((C, ROWS)...]
    unnamed x0 -> x1, local copies, waits for them, and re-layouts: none -> 5.77 us
where the time goes in v3:
time: 104 us
  Pallas kernels  98.2 us (94%)
  local copies, waits for them, and re-layouts  5.77 us (6%)
    pallas_call x1, Pallas kernels, propagate(): pl.pallas_call(propagate_kernel, out_shape=jax.ShapeDtypeStruct((C, ROWS)...  98.2 us
    unnamed x1, local copies, waits for them, and re-layouts  5.77 us

profile of v3, /device:TPU:1, one launch (start us, length us, event | category | flops | bytes accessed | tf_op | source)
XLA Modules:
  0.0 104.0 jit_solution(10728406456967906121)
XLA Ops:
  0.0 98.2 %propagate.1 = f32[172,8192]{1,0:T(8,128)} custom-call(s32[32,128]{1,0:T(8,128)} %bitcast.9, s32[128]{0:T(128)} %cnt_hbm.1, bf16[8192,128]{1,0:T(8,128)(2,1)} %feat_hbm.1, bf16[172,128]{1,0:T(8,128)(2,1)} %bitcast.8, f32[1,172]{1,0:T(1,128)} %bitcast.11, f32[1,172]{1,0:T(1,128)} %bitcast.12, f32[1,172]{1,0:T(1,128)} %bitcast.13, ...), custom_call_target="tpu_custom_call" | custom-call | flops 12884901888 | bytes 25165824 | tf_op jit(solution)/shard_map/propagate/pallas_call | solution.py:330
  98.2 5.8 %copy.12 = f32[8192,172]{0,1:T(8,128)} copy(f32[8192,172]{0,1:T(8,128)} %bitcast.7) | data formatting | bytes 11272192

commit v4 on v3

--- a/solution.py
+++ b/solution.py
@@ -26,7 +26,7 @@
 LOG_FLOOR = 0.0001
 DEAD = 32768.0
 LOW = -1e30
-VMEM_LIMIT = 58 * 2**20
+VMEM_LIMIT = 50 * 2**20
 GANG = 8
 MESH = pl.DeviceIdType.MESH
 MIX = 37
@@ -100,12 +100,15 @@
         lane = lax.broadcasted_iota(jnp.int32, (PACK, HALF), 1)
         return jnp.where(lane < HALF // 2, values[:PACK], pltpu.roll(values[PACK:], HALF // 2, 1))
 
+    def turned(turn, sign):
+        return lax.rem(me + N + sign * lax.rem((turn + 1) * MIX, N), N)
+
     def spread(make, sendbuf, landing, number, first=0, last=N):
-        def gang(base, turns):
-            dests = [lax.rem(me + lax.rem((base + u) * MIX, N), N) for u in turns]
-            for u, dest in zip(turns, dests):
+        def gang(base, size):
+            dests = [turned(base + u, 1) for u in range(size)]
+            for u, dest in enumerate(dests):
                 sendbuf[pl.ds(base + u, 1)] = make(dest)[None]
-            for u, dest in zip(turns, dests):
+            for u, dest in enumerate(dests):
                 pltpu.make_async_remote_copy(
                     src_ref=sendbuf.at[base + u], dst_ref=landing(base + u),
                     send_sem=send_sem.at[number], recv_sem=recv_sem.at[number],
@@ -113,13 +116,14 @@
                 ).start()
 
         def several(i, carry):
-            gang(i * GANG, range(GANG))
+            gang(i * GANG, GANG)
             return carry
 
-        if first == 0:
-            gang(0, range(1, GANG))
-        lax.fori_loop(max(first // GANG, 1), last // GANG, several, 0)
-        whole = sendbuf.at[pl.ds(0, last - max(first, 1))]
+        full = last // GANG - (last == N)
+        lax.fori_loop(first // GANG, full, several, 0)
+        if last == N:
+            gang(full * GANG, GANG - 1)
+        whole = sendbuf.at[pl.ds(0, last - first - (last == N))]
         return pltpu.make_async_remote_copy(
             src_ref=whole, dst_ref=whole, send_sem=send_sem.at[number], recv_sem=recv_sem.at[number],
             device_id=(next_door,), device_id_type=MESH,
@@ -142,6 +146,15 @@
 
     def rows_b(dest):
         return packed(picked(wide_b, dest, 0.0)).astype(BF16)
+
+    def landing(turn):
+        return feat_recv.at[turn]
+
+    feat_recv[pl.ds(N - 1, 1)] = feature_rows(me)[None]
+    pl.semaphore_wait(barrier, N - 1)
+    early = spread(feature_rows, send_a, landing, 0, 0, N // 2)
+    late = spread(feature_rows, send_a, landing, 7, N // 2, N)
+    loads[9].start()
 
     wpad[...] = jnp.zeros_like(wpad)
     wpad[pl.ds(0, C), :] = wt[...].astype(F32)
@@ -166,7 +179,6 @@
         return acc + jnp.sum(p.astype(F32).reshape(CHUNK // 8, 8, CP), axis=0)
 
     acc = lax.fori_loop(0, ROWS // CHUNK, local, jnp.zeros((8, CP), F32))
-    pl.semaphore_wait(barrier, N - 1)
 
     group = me // GROUP
     place = lax.rem(me, GROUP)
@@ -186,11 +198,25 @@
         send_sem=send_sem.at[5], recv_sem=recv_sem.at[5], device_id=(next_door,), device_id_type=MESH,
     )
 
-    def landing(turn):
-        return feat_recv.at[turn]
-
-    feat_recv[pl.ds(0, 1)] = feature_rows(me)[None]
-    early = spread(feature_rows, send_a, landing, 0, 0, N // 2)
+    sources = CHUNK // SLOT
+
+    def boundary(k, carry):
+        f = feat_recv[pl.ds(k * sources, sources)].reshape(CHUNK, F)
+        live = f[:, :1].astype(F32) < DEAD / 2
+        p = jnp.where(live, soft(f), 0.0).astype(BF16)
+        for u in range(sources):
+            source = turned(k * sources + u, -1)
+            block = RB + source // (B // SLOT)
+            row = pl.multiple_of(lax.rem(source, B // SLOT) * SLOT, SLOT)
+            seed_a[pl.ds(block, 1), pl.ds(row, SLOT), :] = p[u * SLOT : (u + 1) * SLOT, :HALF][None]
+            seed_b[pl.ds(block, 1), pl.ds(row, SLOT), :] = p[u * SLOT : (u + 1) * SLOT, HALF:][None]
+        return carry
+
+    turns = N // sources
+    for labels in (seed_a, seed_b, one_a, one_b, two_a, two_b):
+        labels[pl.ds(RB + HB, 1)] = jnp.zeros((1, B, HALF), BF16)
+    early.wait_recv()
+    lax.fori_loop(0, turns // 2, boundary, 0)
     near.wait_recv()
     part2[pl.ds(group, 1)] = jnp.sum(part1[...], axis=0)[None]
 
@@ -206,11 +232,8 @@
         src_ref=part2.at[pl.ds(0, groups - 1)], dst_ref=part2.at[pl.ds(0, groups - 1)],
         send_sem=send_sem.at[6], recv_sem=recv_sem.at[6], device_id=(next_door,), device_id_type=MESH,
     )
-    late = spread(feature_rows, send_a, landing, 7, N // 2, N)
-    loads[9].start()
-    for labels in (seed_a, seed_b, one_a, one_b, two_a, two_b):
-        labels[pl.ds(RB + HB, 1)] = jnp.zeros((1, B, HALF), BF16)
-
+    late.wait_recv()
+    lax.fori_loop(turns // 2, turns, boundary, 0)
     far.wait_recv()
     total = jnp.sum(jnp.sum(part2[...], axis=0), axis=0, keepdims=True)
     ratio = tpad[...] / (MOMENTUM * epad[...] + (1.0 - MOMENTUM) * total / NODES)
@@ -230,31 +253,10 @@
         seed_b[pl.ds(k * blocks, blocks)] = b.reshape(blocks, B, HALF)
         return carry
 
-    lax.fori_loop(0, RB * B // CHUNK, align, 0)
-
-    sources = CHUNK // SLOT
-
-    def boundary(k, carry):
-        f = feat_recv[pl.ds(k * sources, sources)].reshape(CHUNK, F)
-        live = f[:, :1].astype(F32) < DEAD / 2
-        p = jnp.where(live, soft(f), 0.0).astype(BF16)
-        a, b = aligned(p[:, :HALF], p[:, HALF:])
-        for u in range(sources):
-            source = lax.rem(me + N - lax.rem((k * sources + u) * MIX, N), N)
-            block = RB + source // (B // SLOT)
-            row = pl.multiple_of(lax.rem(source, B // SLOT) * SLOT, SLOT)
-            seed_a[pl.ds(block, 1), pl.ds(row, SLOT), :] = a[u * SLOT : (u + 1) * SLOT][None]
-            seed_b[pl.ds(block, 1), pl.ds(row, SLOT), :] = b[u * SLOT : (u + 1) * SLOT][None]
-        return carry
-
-    turns = N // sources
-    early.wait_recv()
-    lax.fori_loop(0, turns // 2, boundary, 0)
-    late.wait_recv()
-    lax.fori_loop(turns // 2, turns, boundary, 0)
+    lax.fori_loop(0, (RB + HB) * B // CHUNK, align, 0)
     loads[9].wait()
 
-    def multiply(labels, seeds, following, wides):
+    def multiply(labels, seeds, following, wides, low=None):
         def several(i, carry):
             for u in range(UNROLL):
                 r = i * UNROLL + u
@@ -271,8 +273,8 @@
                         wides[q][pl.ds(at, B), :] = current
                         following[q][pl.ds(r, 1)] = current.astype(BF16)[None]
                     else:
-                        low, high = q * HALF, min((q + 1) * HALF, C)
-                        out_ref[pl.ds(low, high - low), pl.ds(at, B)] = jnp.log(current.T[: high - low] + LOG_FLOOR)
+                        classes = min(HALF, C - low)
+                        out_ref[pl.ds(low, classes), pl.ds(at, B)] = jnp.log(current.T[:classes] + LOG_FLOOR)
             return carry
 
         lax.fori_loop(0, RB // UNROLL, several, 0)
@@ -295,28 +297,29 @@
     multiply((seed_a, seed_b), (seed_a, seed_b), (one_a, one_b), (wide_a, wide_b))
     early.wait_send()
     late.wait_send()
+    recv_b1[pl.ds(me, 1)] = rows_b(me)[None]
+    sent_b1 = spread(rows_b, send_b, here(recv_b1), 2)
     put_own(one_a, rows_a(me))
     sent_a1 = spread(rows_a, send_a, own_place(one_a), 1)
-    recv_b1[pl.ds(me, 1)] = rows_b(me)[None]
-    sent_b1 = spread(rows_b, send_b, here(recv_b1), 2)
-
-    sent_a1.wait_recv()
-    multiply((one_a,), (seed_a,), (two_a,), (wide_a,))
-    sent_a1.wait_send()
-    put_own(two_a, rows_a(me))
-    sent_a2 = spread(rows_a, send_a, own_place(two_a), 3)
+
     sent_b1.wait_recv()
     unpack(recv_b1, one_b)
     multiply((one_b,), (seed_b,), (two_b,), (wide_b,))
     sent_b1.wait_send()
     recv_b2[pl.ds(me, 1)] = rows_b(me)[None]
     sent_b2 = spread(rows_b, send_b, here(recv_b2), 4)
-
-    sent_a2.wait_recv()
+    sent_a1.wait_recv()
+    multiply((one_a,), (seed_a,), (two_a,), (wide_a,))
+    sent_a1.wait_send()
+    put_own(two_a, rows_a(me))
+    sent_a2 = spread(rows_a, send_a, own_place(two_a), 3)
+
     sent_b2.wait_recv()
     unpack(recv_b2, two_b)
-    multiply((two_a, two_b), (seed_a, seed_b), (), ())
-    for sent in (near, far, sent_a2, sent_b2):
+    multiply((two_b,), (seed_b,), (), (), HALF)
+    sent_a2.wait_recv()
+    multiply((two_a,), (seed_a,), (), (), 0)
+    for sent in (near, far, sent_b2, sent_a2):
         sent.wait_send()
 
 
@@ -329,7 +332,7 @@
     vector = pltpu.VMEM((1, C), F32)
     return pl.pallas_call(
         propagate_kernel,
-        out_shape=jax.ShapeDtypeStruct((C, ROWS), F32),
+        out_shape=pltpu.VMEM((C, ROWS), F32),
         in_specs=[in_hbm()] * 10,
         out_specs=in_vmem(),
         scratch_shapes=[
@@ -360,7 +363,7 @@
             flops=6 * RB * TPR * B * B * CP, bytes_accessed=24 * 2**20, transcendentals=(ROWS + HB * B) * CP
         ),
         name="propagate",
-    )(rows_t, counts, features, wt, bias, ema, target, tiles, cols_t, used)
+    )(*[pltpu.with_memory_space_constraint(x, pltpu.HBM) for x in (rows_t, counts, features, wt, bias, ema, target, tiles, cols_t, used)])
 
 
 def on_device(

time: 104 us -> 95.3 us (0.916)
  Pallas kernels: 98.2 us -> 92.7 us
  local copies, waits for them, and re-layouts: 5.77 us -> 2.53 us
    pallas_call x1, Pallas kernels: 98.2 us -> 92.7 us  [propagate(): pl.pallas_call(propagate_kernel, out_shape=pltpu.VMEM((C, ROWS), F32), in...]
    unnamed x1, local copies, waits for them, and re-layouts: 5.77 us -> 2.53 us
where the time goes in v4:
time: 95.3 us; the launch traced here: 95.2 us
  Pallas kernels  92.7 us (97%)
  local copies, waits for them, and re-layouts  2.53 us (3%)
    pallas_call x1, Pallas kernels, propagate(): pl.pallas_call(propagate_kernel, out_shape=pltpu.VMEM((C, ROWS), F32), in...  92.7 us
    unnamed x1, local copies, waits for them, and re-layouts  2.53 us

profile of v4, /device:TPU:1, one launch (start us, length us, event | category | flops | bytes accessed | tf_op | source)
XLA Modules:
  0.0 95.2 jit_solution(11407495250865019483)
XLA Ops:
  0.0 92.7 %propagate.1 = f32[172,8192]{1,0:T(8,128)S(1)} custom-call(s32[32,128]{1,0:T(8,128)} %bitcast.9, s32[128]{0:T(128)} %cnt_hbm.1, bf16[8192,128]{1,0:T(8,128)(2,1)} %feat_hbm.1, bf16[172,128]{1,0:T(8,128)(2,1)} %bitcast.8, f32[1,172]{1,0:T(1,128)} %bitcast.11, f32[1,172]{1,0:T(1,128)} %bitcast.12, f32[1,172]{1,0:T(1,128)} %bitcast.13, ...), custom_call_target="tpu_custom_call" | custom-call | flops 12884901888 | bytes 25165824 | tf_op jit(solution)/shard_map/propagate/pallas_call | solution.py:333
  92.7 2.5 %copy.12 = f32[8192,172]{0,1:T(8,128)} copy(f32[8192,172]{0,1:T(8,128)S(1)} %bitcast.7) | data formatting | bytes 11272192

commit v5 on v4

--- a/solution.py
+++ b/solution.py
@@ -15,7 +15,7 @@
 HALF = 128
 PACK = 16
 CHUNK = 1024
-UNROLL = 8
+UNROLL = 16
 HB = 32
 ROWS = 8192
 N = 128
@@ -26,10 +26,11 @@
 LOG_FLOOR = 0.0001
 DEAD = 32768.0
 LOW = -1e30
-VMEM_LIMIT = 50 * 2**20
+VMEM_LIMIT = 54 * 2**20
 GANG = 8
 MESH = pl.DeviceIdType.MESH
 MIX = 37
+EARLY = 96
 GROUP = 16
 F32 = jnp.float32
 BF16 = jnp.bfloat16
@@ -152,8 +153,7 @@
 
     feat_recv[pl.ds(N - 1, 1)] = feature_rows(me)[None]
     pl.semaphore_wait(barrier, N - 1)
-    early = spread(feature_rows, send_a, landing, 0, 0, N // 2)
-    late = spread(feature_rows, send_a, landing, 7, N // 2, N)
+    early = spread(feature_rows, send_a, landing, 0, 0, EARLY)
     loads[9].start()
 
     wpad[...] = jnp.zeros_like(wpad)
@@ -193,6 +193,7 @@
         return carry
 
     lax.fori_loop(1, GROUP, send_near, 0)
+    late = spread(feature_rows, send_a, landing, 7, EARLY, N)
     near = pltpu.make_async_remote_copy(
         src_ref=part1.at[pl.ds(0, GROUP - 1)], dst_ref=part1.at[pl.ds(0, GROUP - 1)],
         send_sem=send_sem.at[5], recv_sem=recv_sem.at[5], device_id=(next_door,), device_id_type=MESH,
@@ -212,11 +213,8 @@
             seed_b[pl.ds(block, 1), pl.ds(row, SLOT), :] = p[u * SLOT : (u + 1) * SLOT, HALF:][None]
         return carry
 
-    turns = N // sources
     for labels in (seed_a, seed_b, one_a, one_b, two_a, two_b):
         labels[pl.ds(RB + HB, 1)] = jnp.zeros((1, B, HALF), BF16)
-    early.wait_recv()
-    lax.fori_loop(0, turns // 2, boundary, 0)
     near.wait_recv()
     part2[pl.ds(group, 1)] = jnp.sum(part1[...], axis=0)[None]
 
@@ -232,8 +230,8 @@
         src_ref=part2.at[pl.ds(0, groups - 1)], dst_ref=part2.at[pl.ds(0, groups - 1)],
         send_sem=send_sem.at[6], recv_sem=recv_sem.at[6], device_id=(next_door,), device_id_type=MESH,
     )
-    late.wait_recv()
-    lax.fori_loop(turns // 2, turns, boundary, 0)
+    early.wait_recv()
+    lax.fori_loop(0, EARLY // sources, boundary, 0)
     far.wait_recv()
     total = jnp.sum(jnp.sum(part2[...], axis=0), axis=0, keepdims=True)
     ratio = tpad[...] / (MOMENTUM * epad[...] + (1.0 - MOMENTUM) * total / NODES)
@@ -253,7 +251,10 @@
         seed_b[pl.ds(k * blocks, blocks)] = b.reshape(blocks, B, HALF)
         return carry
 
-    lax.fori_loop(0, (RB + HB) * B // CHUNK, align, 0)
+    lax.fori_loop(0, RB * B // CHUNK, align, 0)
+    late.wait_recv()
+    lax.fori_loop(EARLY // sources, N // sources, boundary, 0)
+    lax.fori_loop(RB * B // CHUNK, (RB + HB) * B // CHUNK, align, 0)
     loads[9].wait()
 
     def multiply(labels, seeds, following, wides, low=None):

time: 95.3 us -> 92.1 us (0.966)
  Pallas kernels: 92.7 us -> 89.4 us
    pallas_call x1, Pallas kernels: 92.7 us -> 89.4 us  [propagate(): pl.pallas_call(propagate_kernel, out_shape=pltpu.VMEM((C, ROWS), F32), in...]
where the time goes in v5:
time: 92.1 us; the launch traced here: 92 us
  Pallas kernels  89.4 us (97%)
  local copies, waits for them, and re-layouts  2.53 us (3%)
    pallas_call x1, Pallas kernels, propagate(): pl.pallas_call(propagate_kernel, out_shape=pltpu.VMEM((C, ROWS), F32), in...  89.4 us
    unnamed x1, local copies, waits for them, and re-layouts  2.53 us

profile of v5, /device:TPU:1, one launch (start us, length us, event | category | flops | bytes accessed | tf_op | source)
XLA Modules:
  0.0 92.0 jit_solution(15328968155059894656)
XLA Ops:
  0.0 89.4 %propagate.1 = f32[172,8192]{1,0:T(8,128)S(1)} custom-call(s32[32,128]{1,0:T(8,128)} %bitcast.9, s32[128]{0:T(128)} %cnt_hbm.1, bf16[8192,128]{1,0:T(8,128)(2,1)} %feat_hbm.1, bf16[172,128]{1,0:T(8,128)(2,1)} %bitcast.8, f32[1,172]{1,0:T(1,128)} %bitcast.11, f32[1,172]{1,0:T(1,128)} %bitcast.12, f32[1,172]{1,0:T(1,128)} %bitcast.13, ...), custom_call_target="tpu_custom_call" | custom-call | flops 12884901888 | bytes 25165824 | tf_op jit(solution)/shard_map/propagate/pallas_call | solution.py:334
  89.4 2.5 %copy.12 = f32[8192,172]{0,1:T(8,128)} copy(f32[8192,172]{0,1:T(8,128)S(1)} %bitcast.7) | data formatting | bytes 11272192
